TPU v7x, 32 devices: a whole 2x2x4 slice. The times are simulated.
32 devices in a mesh: groups: 2 (over y), replica: 2 (over core), tensor: 8 (over z, x).
Axes of the slice: x: 2, y: 2, z: 4, core: 2. Of those that a mesh axis runs over, the one named last changes fastest.
Arguments:
- tokens: bfloat16 [2560, 8192], P(('groups', 'replica', 'tensor')), parts along dimension 0, may hold values from -6 to 6, as said below
- norm_scale_weight: float32 [8192], replicated, may hold values from 0.25 to 1.75
- query_weight: bfloat16 [128, 4096, 128], P('tensor'), may hold values from -0.06629126 to 0.06629126, as said below
- key_value_weight: bfloat16 [1024, 2, 8192], P('tensor'), may hold values from -0.06629126 to 0.06629126, as said below
- adapter_down_weight: bfloat16 [96, 8192, 128], P('replica', 'tensor'), may hold values from -0.0625 to 0.0625
- adapter_up_query: bfloat16 [96, 128, 32, 128], P('replica', 'tensor'), may hold values from -0.75 to 0.75
- adapter_up_value: bfloat16 [96, 65536], P('replica', 'tensor'), may hold values from -0.75 to 0.75
- request_adapter_index: int32 [4, 8], P('groups'), parts along dimension 0, may hold values from 0 to 95
- adapter_slot: int32 [96], replicated, may hold values from 0 to 95, each once
- request_row_lengths: int32 [4, 8], P('groups'), parts along dimension 0, may hold values from 1 to 160, 640 in all within a row
Outputs:
- context: bfloat16 [4, 128, 320, 128], P(('groups', 'replica'), 'tensor'), parts along dimension 0
There are 2 independent parts, one for each index of `groups`. A program takes and returns all parts, laid end to end along the dimension named above; an argument that names none is the same for every part. Nothing has to cross between parts.
Inputs may be any that keep to these rules, and one draw needn't show every extreme that they name: `request_adapter_index`: the adapter that each request uses; adapters may repeat. A permutation: adapter a is stored in slot adapter_slot[a], and slots r * 48 to (r + 1) * 48 - 1 are held by replica r. `request_row_lengths`: each row sums to 640; the requests of a replica cover its rows in order. `tokens`: drawn afresh for each group. `query_weight`: shared by all groups. `key_value_weight`: shared by all groups.
All inputs are finite; a program needn't handle non-finite values.
Results may differ from a plain program's by a relative error of at most 0.0092.
Values may be sent and summed in bfloat16 or wider, within the bound.
A program may use at most 192 MiB of HBM per device.

v0:
```python
import math

import jax
import jax.numpy as jnp
from jax import lax
from jax.experimental import pallas as pl
from jax.experimental.pallas import tpu as pltpu
from jax.sharding import PartitionSpec as P

QUERY_HEADS = 64
KEYVALUE_HEADS = 8
HEAD_WIDTH = 128


def partner_2(block, axis, apart):
    count = lax.axis_size(axis)
    route = []
    for low in range(count):
        high = low | 1 << apart
        if high != low and high < count:
            route += [(low, high), (high, low)]
    return lax.ppermute(block, axis, route)


def on_device(
    tokens,
    norm_scale_weight,
    query_weight,
    key_value_weight,
    adapter_down_weight,
    adapter_up_query,
    adapter_up_value,
    request_adapter_index,
    adapter_slot,
    request_row_lengths,
):
    shards = lax.axis_size("tensor")
    position = lax.axis_index("tensor")
    replica_now = lax.axis_index("replica")
    local_columns = adapter_down_weight.shape[1]
    complete_rank = adapter_down_weight.shape[2] // 2
    head_rows = query_weight.shape[0]
    half_width = query_weight.shape[1]
    head_length = query_weight.shape[2]
    half_rank_count = adapter_up_query.shape[2]
    value_cols = key_value_weight.shape[0]
    top_bit = shards.bit_length() - 2
    side = position // (shards // 2)
    first_head = position * head_rows - side * QUERY_HEADS
    widened = tokens.astype(jnp.float32)
    normed = (
        widened
        * lax.rsqrt(jnp.mean(widened * widened, axis=1, keepdims=True) + 1e-05)
        * norm_scale_weight
    ).astype(jnp.bfloat16)
    gathered_rows = lax.all_gather(normed, "tensor", axis=0, tiled=True)
    length_gathered = gathered_rows.shape[0]
    lengths_mine = lax.dynamic_index_in_dim(request_row_lengths, replica_now, 0, keepdims=False)
    seg_ends = jnp.cumsum(lengths_mine)
    seg_starts = seg_ends - lengths_mine
    row_index = jnp.arange(length_gathered, dtype=jnp.int32)
    member_mask = (row_index[:, None] >= seg_starts[None, :]) & (
        row_index[:, None] < seg_ends[None, :]
    )
    member_bf = member_mask.astype(jnp.bfloat16)
    segment_ids = jnp.sum((row_index[:, None] >= seg_ends[None, :]).astype(jnp.int32), axis=1)
    wanted = lax.dynamic_index_in_dim(request_adapter_index, replica_now, 0, keepdims=False)
    storage_slots = jnp.take(adapter_slot, wanted)
    gathered = (
        lax.all_gather(adapter_down_weight, "replica", axis=0, tiled=True),
        lax.all_gather(adapter_up_query, "replica", axis=0, tiled=True),
        lax.all_gather(adapter_up_value, "replica", axis=0, tiled=True),
    )
    fetched = tuple((jnp.take(store_part, storage_slots, axis=0) for store_part in gathered))
    down_sel, upq_sel, upv_sel = fetched
    requests = down_sel.shape[0]
    my_columns = lax.dynamic_slice_in_dim(gathered_rows, position * local_columns, local_columns, 1)
    down_mat = jnp.transpose(down_sel, (1, 0, 2)).reshape(
        local_columns, requests * 2 * complete_rank
    )
    per_request = jnp.dot(my_columns, down_mat, preferred_element_type=jnp.float32).reshape(
        length_gathered, requests, 2 * complete_rank
    )
    partial_down = jnp.sum(
        jnp.where(member_mask[:, :, None], per_request, jnp.float32(0.0)), axis=1
    )
    down_bf = lax.psum(partial_down, "tensor").astype(jnp.bfloat16)
    down_query = lax.dynamic_slice_in_dim(down_bf, side * half_rank_count, half_rank_count, 1)
    down_value = down_bf[:, complete_rank:]
    expand_query = (member_bf[:, :, None] * down_query[:, None, :]).reshape(
        length_gathered, requests * half_rank_count
    )
    upq_mat = jnp.transpose(upq_sel, (1, 0, 2, 3)).reshape(
        head_rows, requests * half_rank_count, head_length
    )
    my_features = lax.dynamic_slice_in_dim(gathered_rows, side * half_width, half_width, 1)
    partial_query = jnp.einsum(
        "tf,mfd->mtd", my_features, query_weight, preferred_element_type=jnp.float32
    )
    partial_query = partial_query + jnp.einsum(
        "tj,mjd->mtd", expand_query, upq_mat, preferred_element_type=jnp.float32
    )
    partner = partner_2(partial_query, "tensor", top_bit)
    query_all = (partial_query + partner).astype(jnp.bfloat16)
    kv_local = jnp.einsum(
        "ckf,tf->ckt", key_value_weight, gathered_rows, preferred_element_type=jnp.float32
    )
    expand_value = (member_bf[:, :, None] * down_value[:, None, :]).reshape(
        length_gathered, requests * complete_rank
    )
    upv_mat = jnp.transpose(
        upv_sel.reshape(requests, value_cols, complete_rank), (1, 0, 2)
    ).reshape(value_cols, requests * complete_rank)
    value_term = jnp.einsum("cj,tj->ct", upv_mat, expand_value, preferred_element_type=jnp.float32)
    key_value = jnp.stack([kv_local[:, 0], kv_local[:, 1] + value_term], axis=1).astype(
        jnp.bfloat16
    )
    key_value_gathered = lax.all_gather(key_value, "tensor", axis=0, tiled=True)
    key_value_heads = key_value_gathered.reshape(KEYVALUE_HEADS, head_length, 2, length_gathered)
    group_width = QUERY_HEADS // KEYVALUE_HEADS
    head_ids = (first_head + jnp.arange(head_rows, dtype=jnp.int32)) // group_width
    chosen_heads = jnp.take(key_value_heads, head_ids, axis=0)
    key_head_count = chosen_heads[:, :, 0]
    value_head_count = chosen_heads[:, :, 1]
    rows_here = length_gathered // 2
    query_seq = lax.dynamic_slice_in_dim(query_all, side * rows_here, rows_here, 1)
    query_index = side * rows_here + jnp.arange(rows_here, dtype=jnp.int32)
    query_segment = jnp.take(segment_ids, query_index)
    allowed = (row_index[None, :] <= query_index[:, None]) & (
        segment_ids[None, :] == query_segment[:, None]
    )
    scores = jnp.einsum(
        "mqd,mdk->mqk", query_seq, key_head_count, preferred_element_type=jnp.float32
    ) / math.sqrt(HEAD_WIDTH)
    scores = jnp.where(allowed[None], scores, jnp.float32(-1e30))
    row_max = jnp.max(scores, axis=-1, keepdims=True)
    weights = jnp.exp(scores - row_max)
    weights = (weights / jnp.sum(weights, axis=-1, keepdims=True)).astype(jnp.bfloat16)
    context = jnp.einsum(
        "mqk,mdk->mqd", weights, value_head_count, preferred_element_type=jnp.float32
    )
    return context[None].astype(jnp.bfloat16)


def swap(block, bit):
    return partner_2(block, "tensor", bit)


def side_gather(block, index):
    count, rest = block.shape[0], block.shape[1:]
    half = count // 2
    near = swap(block, 0)
    far = swap(block, 1)
    across = jnp.concatenate([swap(near[:half], 1), swap(far[half:], 0)], axis=0)
    result = jnp.zeros((4 * count,) + rest, block.dtype)
    for mask, piece in enumerate((block, near, far, across)):
        result = lax.dynamic_update_slice_in_dim(result, piece, (index ^ mask) * count, 0)
    return result, near


def after(block, earlier):
    return block + earlier[0, 0] * jnp.zeros((), block.dtype)


def pick_kernel(wanted, slot, *refs):
    stores, outs, sems = refs[:3], refs[3:9], refs[9]
    replica = lax.axis_index("replica")
    held = stores[0].shape[0]
    copies = []
    for which in range(2):
        whose = replica if which else 1 - replica
        for request in range(outs[0].shape[0]):
            local = jnp.clip(slot[wanted[whose, request]] - replica * held, 0, held - 1)
            for store in range(3):
                copy = pltpu.make_async_copy(
                    stores[store].at[pl.ds(local, 1)],
                    outs[which * 3 + store].at[pl.ds(request, 1)],
                    sems.at[len(copies)],
                )
                copy.start()
                copies.append(copy)
    for copy in copies:
        copy.wait()


def fetch_adapters(stores, wanted_pair, adapter_slot, replica_now):
    held = stores[0].shape[0]
    count = wanted_pair.shape[1]
    smem, anywhere = pl.BlockSpec(memory_space=pltpu.SMEM), pl.BlockSpec(memory_space=pl.ANY)
    picked = pl.pallas_call(
        pick_kernel,
        out_shape=[jax.ShapeDtypeStruct((count,) + x.shape[1:], x.dtype) for x in stores] * 2,
        in_specs=[smem, smem] + [anywhere] * 3,
        out_specs=[pl.BlockSpec(memory_space=pltpu.VMEM)] * 6,
        compiler_params=pltpu.CompilerParams(vmem_limit_bytes=24 * 1024 * 1024),
        scratch_shapes=[pltpu.SemaphoreType.DMA((count * 6,))],
    )(wanted_pair, adapter_slot, *stores)
    mine = jnp.take(adapter_slot, lax.dynamic_index_in_dim(wanted_pair, replica_now, 0, keepdims=False))
    base = replica_now * held
    here = (mine >= base) & (mine < base + held)
    result = []
    for theirs, own in zip(picked[:3], picked[3:]):
        received = lax.ppermute(theirs, "replica", [(0, 1), (1, 0)])
        keep = here.reshape((count,) + (1,) * (own.ndim - 1))
        result.append(jnp.where(keep, own, received))
    return result


def on_square(
    tokens,
    norm_scale_weight,
    query_weight,
    key_value_weight,
    adapter_down_weight,
    adapter_up_query,
    adapter_up_value,
    request_adapter_index,
    adapter_slot,
    request_row_lengths,
):
    f32, bf = jnp.float32, jnp.bfloat16
    position = lax.axis_index("tensor")
    replica_now = lax.axis_index("replica")
    side, index = position // 4, position % 4
    rows = tokens.shape[0]
    side_rows = 4 * rows
    all_rows = 2 * side_rows
    window = all_rows // 4
    half_width = query_weight.shape[1]
    head_rows = query_weight.shape[0]
    local_columns = adapter_down_weight.shape[1]
    rank = adapter_down_weight.shape[2] // 2
    half_rank = adapter_up_query.shape[2]

    widened = tokens.astype(f32)
    normed = (
        widened
        * lax.rsqrt(jnp.mean(widened * widened, axis=1, keepdims=True) + 1e-05)
        * norm_scale_weight
    ).astype(bf)
    near_half = lax.dynamic_slice_in_dim(normed, side * half_width, half_width, 1)
    far_half = lax.dynamic_slice_in_dim(normed, (1 - side) * half_width, half_width, 1)
    other_near = swap(far_half, 2)
    own_near_all, first_in = side_gather(near_half, index)
    zero = (first_in[0, 0] * jnp.zeros((), bf)).astype(jnp.int32)
    other_near_all, _ = side_gather(other_near, index)
    other_far = swap(after(near_half, other_near), 2)

    down_sel, upq_sel, upv_sel = fetch_adapters(
        (
            adapter_down_weight,
            adapter_up_query,
            adapter_up_value.reshape(adapter_up_value.shape[0], -1, HEAD_WIDTH),
        ),
        request_adapter_index + zero,
        adapter_slot,
        replica_now,
    )
    requests = down_sel.shape[0]

    lengths_mine = lax.dynamic_index_in_dim(request_row_lengths, replica_now, 0, keepdims=False)
    seg_ends = jnp.cumsum(lengths_mine)
    seg_starts = seg_ends - lengths_mine

    def members(index_of):
        return (index_of[:, None] >= seg_starts[None, :]) & (index_of[:, None] < seg_ends[None, :])

    line = jnp.arange(side_rows, dtype=jnp.int32)
    own_index = side * side_rows + line
    other_index = (1 - side) * side_rows + line
    own_member, other_member = members(own_index), members(other_index)

    down_mat = jnp.transpose(down_sel, (1, 0, 2)).reshape(local_columns, requests * 2 * rank)

    def down_part(gathered, member):
        mine = lax.dynamic_slice_in_dim(gathered, index * local_columns, local_columns, 1)
        each = jnp.dot(mine, down_mat, preferred_element_type=f32).reshape(
            side_rows, requests, 2 * rank
        )
        return jnp.sum(jnp.where(member[:, :, None], each, f32(0.0)), axis=1)

    down_own = down_part(own_near_all, own_member)
    down_other = down_part(other_near_all, other_member)
    crossed = swap(jnp.stack([down_other, down_own], axis=0), 2)
    down = jnp.stack([down_own, down_other], axis=0) + crossed
    own_far_all, last = side_gather(after(far_half, crossed[0].astype(bf)), index)
    other_far_all, _ = side_gather(after(other_far, last), index)
    down = down + swap(down, 1)
    down = (down + swap(down, 0)).astype(bf)

    def expand(member, values):
        return (member.astype(bf)[:, :, None] * values[:, None, :]).reshape(
            values.shape[0], requests * values.shape[1]
        )

    def up_matrix(selected):
        return jnp.transpose(selected, (1, 0, 2, 3)).reshape(
            head_rows, requests * half_rank, HEAD_WIDTH
        )

    upq_mat = up_matrix(upq_sel)

    def query_base(gathered):
        return lax.optimization_barrier(
            jnp.einsum("tf,mfd->mtd", gathered, query_weight, preferred_element_type=f32)
        )

    def query_part(base, member, down_rows):
        ranks = lax.dynamic_slice_in_dim(down_rows, side * half_rank, half_rank, 1)
        return base + jnp.einsum(
            "tj,mjd->mtd", expand(member, ranks), upq_mat, preferred_element_type=f32
        )

    received = swap(query_part(query_base(other_near_all), other_member, down[1]).astype(bf), 2)
    own_query = query_part(query_base(own_near_all), own_member, down[0])
    query = (own_query + received.astype(f32)).astype(bf)

    kv_near = lax.dynamic_slice_in_dim(key_value_weight, (side + zero) * half_width, half_width, 2)
    kv_far = lax.dynamic_slice_in_dim(key_value_weight, (1 - side + zero) * half_width, half_width, 2)
    upv_mat = jnp.transpose(
        upv_sel.reshape(requests, HEAD_WIDTH, rank), (0, 2, 1)
    ).reshape(requests * rank, HEAD_WIDTH)

    def key_values(near, far, member, down_value):
        base = jnp.einsum("tf,ckf->ktc", near, kv_near, preferred_element_type=f32) + jnp.einsum(
            "tf,ckf->ktc", far, kv_far, preferred_element_type=f32
        )
        up = jnp.dot(expand(member, down_value), upv_mat, preferred_element_type=f32)
        return jnp.stack([base[0], base[1] + up], axis=0).astype(bf)

    kv_own = key_values(own_near_all, own_far_all, own_member, down[0, :, rank:])
    kv_other = key_values(other_near_all, other_far_all, other_member, down[1, :, rank:])
    kv_rows = jnp.zeros((2, window + all_rows, HEAD_WIDTH), bf)
    kv_rows = lax.dynamic_update_slice_in_dim(kv_rows, kv_own, window + side * side_rows, 1)
    kv_rows = lax.dynamic_update_slice_in_dim(kv_rows, kv_other, window + (1 - side) * side_rows, 1)
    span = window + side_rows
    for_low, for_high = kv_rows[:, :span], kv_rows[:, side_rows:]
    odd = position % 2 == 1
    first = lax.ppermute(
        jnp.where(odd, for_high, for_low), "tensor", [(c, c // 2 + 4 * (c % 2)) for c in range(8)]
    )
    second = lax.ppermute(
        jnp.where(odd, for_low, for_high), "tensor", [(c, c // 2 + 4 * (1 - c % 2)) for c in range(8)]
    )
    even_kv = jnp.where(side == 0, first, second)
    odd_kv = jnp.where(side == 0, second, first)
    kv = jnp.stack([even_kv, odd_kv], axis=0)

    blocks = side_rows // window
    kv = jnp.stack([kv[:, :, b * window : (b + 2) * window] for b in range(blocks)], axis=1)
    query_index = own_index.reshape(blocks, window)
    key_index = jnp.stack(
        [side * side_rows + (b - 1) * window + jnp.arange(2 * window, dtype=jnp.int32) for b in range(blocks)]
    )

    def segment(index_of):
        return jnp.sum((index_of[..., None] >= seg_ends).astype(jnp.int32), axis=-1)

    allowed = (
        (key_index[:, None, :] >= 0)
        & (key_index[:, None, :] <= query_index[:, :, None])
        & (segment(key_index)[:, None, :] == segment(query_index)[:, :, None])
    )
    query = query.reshape(2, head_rows // 2, blocks, window, HEAD_WIDTH)
    scores = jnp.einsum(
        "ghbqd,gbkd->gbhqk", query, kv[:, :, 0], preferred_element_type=f32
    ) / math.sqrt(HEAD_WIDTH)
    scores = jnp.where(allowed[None, :, None], scores, f32(-1e30))
    row_max = jnp.max(scores, axis=-1, keepdims=True)
    weights = jnp.exp(scores - row_max)
    weights = (weights / jnp.sum(weights, axis=-1, keepdims=True)).astype(bf)
    context = jnp.einsum("gbhqk,gbkd->ghbqd", weights, kv[:, :, 1], preferred_element_type=f32)
    return context.reshape(1, head_rows, side_rows, HEAD_WIDTH).astype(bf)


def solution(mesh):
    square = mesh.shape["tensor"] == KEYVALUE_HEADS
    in_specs = (
        P(("groups", "replica", "tensor"), None),
        P(),
        P("tensor", None, None),
        P("tensor", None, None),
        P("replica", "tensor", None),
        P("replica", "tensor", None, None),
        P("replica", "tensor"),
        P("groups", None),
        P(),
        P("groups", None),
    )
    out_specs = P(("groups", "replica"), "tensor", None, None)
    return jax.shard_map(
        on_square if square else on_device, mesh=mesh, in_specs=in_specs, out_specs=out_specs, check_vma=False
    )
```

profile of v0, /device:TPU:12, one launch (start us, length us, event | category | flops | bytes accessed | tf_op | source)
XLA Modules:
  0.0 286.1 jit_solution(7187724742539508655)
XLA Ops:
  4.5 2.6 collective-permute-start.4
  9.3 26.0 %collective-permute-done.4 = bf16[80,4096]{1,0:T(8,128)(2,1)} collective-permute-done((bf16[80,4096]{1,0:T(8,128)(2,1)}, bf16[80,4096]{1,0:T(8,128)(2,1)}, u32[]{:S(2)}, u32[]{:S(2)}) %collective-permute-start.4) | collective-permute-done | bytes 655392 | tf_op jit(solution)/shard_map/ppermute | solution.py:22
  41.1 1.9 broadcast.307.clone
  43.1 2.0 constant_dynamic-update-slice_fusion.11
  48.1 2.0 constant_dynamic-update-slice_fusion.8
  50.0 6.0 %collective-permute-done = bf16[80,4096]{1,0:T(8,128)(2,1)S(1)} collective-permute-done((bf16[80,4096]{1,0:T(8,128)(2,1)}, bf16[80,4096]{1,0:T(8,128)(2,1)S(1)}, u32[]{:S(2)}, u32[]{:S(2)}) %collective-permute-start) | collective-permute-done | bytes 655392 | tf_op jit(solution)/shard_map/ppermute | solution.py:22
  57.3 4.6 %copy-done.1 = bf16[48,1024,128]{2,1,0:T(8,128)(2,1)S(1)} copy-done((bf16[48,1024,128]{2,1,0:T(8,128)(2,1)S(1)}, bf16[48,1024,128]{2,1,0:T(8,128)(2,1)}, u32[]{:S(2)}) %copy-start.1) | copy-done | bytes 12582936
  61.9 2.8 copy-done.2
  64.7 6.1 %shard_map.100 = (bf16[8,1024,128]{2,1,0:T(8,128)(2,1)}, bf16[8,16,32,128]{3,2,1,0:T(8,128)(2,1)S(1)}, bf16[8,64,128]{2,1,0:T(8,128)(2,1)S(1)}, bf16[8,1024,128]...) custom-call(s32[2,8]{1,0:T(2,128)S(1)} %broadcast_add_fusion.3.wanted, ...), custom_call_target="tpu_custom_call" | custom-call | tf_op jit(solution)/shard_map/pallas_call | solution.py:190
  80.8 2.0 constant_dynamic-update-slice_fusion.7
  83.7 2.0 constant_dynamic-update-slice_fusion.9
  86.8 8.4 %constant_dynamic-slice_fusion.6 = (bf16[128,2,4096]{2,1,0:T(2,128)(2,1)}, bf16[128,2,4096]{2,1,0:T(2,128)(2,1)}) fusion(bf16[128,2,8192]{2,1,0:T(2,128)(2,1)} %param.13, s32[]{:T(128)S(6)} %select_n.156, s32[]{:T(128)S(6)} %select_n.162), kind=kLoop, calls=%fused_computation.152 | loop fusion | bytes 8388616 | tf_op jit(solution)/shard_map/dynamic_slice | solution.py:318
  101.1 3.4 %collective-permute-start.18 = (bf16[80,4096]{1,0:T(8,128)(2,1)}, bf16[80,4096]{1,0:T(8,128)(2,1)}, u32[]{:S(2)}, u32[]{:S(2)}) collective-permute-start(bf16[80,4096]{1,0:T(8,128)(2,1)} %get-tuple-element.19), channel_id=1, source_target_pairs={{0,4},{4,0},{1,5},{5,1},{2,6},{6,2},{3,7},{7,3},{8,12},{12,8},{9,1... | collective-permute-start | bytes 1966088 | tf_op jit(solution)/shard_map/ppermute | solution.py:22
  104.5 4.7 %collective-permute-done.8 = bf16[40,4096]{1,0:T(8,128)(2,1)} collective-permute-done((bf16[40,4096]{1,0:T(8,128)(2,1)}, bf16[40,4096]{1,0:T(8,128)(2,1)}, u32[]{:S(2)}, u32[]{:S(2)}) %collective-permute-start.8) | collective-permute-done | bytes 327712 | tf_op jit(solution)/shard_map/ppermute | solution.py:22
  109.2 2.5 maximum_dynamic-update-slice_fusion
  111.7 3.2 %select_bitcast_fusion = bf16[1024,8,128]{2,0,1:T(8,128)(2,1)} fusion(bf16[8,1024,128]{2,1,0:T(8,128)(2,1)S(1)} %copy-done.4, bf16[8,1024,128]{2,1,0:T(8,128)(2,1)} %collective-permute-done.9, pred[8]{0:T(512)(128)(4,1)S(1)} %compare_and_fusion.3), kind=kLoop, calls=%fused_computation.37 | loop fusion | flops 1048576 | bytes 6291464 | tf_op jit(solution)/shard_map/transpose | solution.py:273
  114.9 2.9 copy.38
  117.8 2.2 fusion.51
  120.0 2.4 fusion.48
  122.5 3.4 %collective-permute-start.10 = (f32[2,320,128]{2,1,0:T(8,128)S(1)}, f32[2,320,128]{2,1,0:T(8,128)S(1)}, u32[]{:S(2)}, u32[]{:S(2)}) collective-permute-start(f32[2,320,128]{2,1,0:T(8,128)S(1)} %pad_maximum_fusion.2), channel_id=1, source_target_pairs={{0,4},{4,0},{1,5},{5,1},{2,6},{6,2},{3,7},{7,3},{8,12},{12,8},{9,1... | collective-permute-start | bytes 983048 | tf_op jit(solution)/shard_map/ppermute | solution.py:22
  125.9 11.2 %fusion.37 = f32[16,320,128]{2,1,0:T(8,128)} fusion(bf16[16,4096,128]{2,1,0:T(8,128)(2,1)} %param.12, bf16[320,4096]{1,0:T(8,128)(2,1)} %get-tuple-element.46), kind=kOutput, calls=%fused_computation.43 | convolution fusion | flops 5368709120 | bytes 22020096 | tf_op jit(solution)/shard_map/tf,mfd->mtd/dot_general | solution.py:305
  137.1 9.3 %collective-permute-done.10 = f32[2,320,128]{2,1,0:T(8,128)S(1)} collective-permute-done((f32[2,320,128]{2,1,0:T(8,128)S(1)}, f32[2,320,128]{2,1,0:T(8,128)S(1)}, u32[]{:S(2)}, u32[]{:S(2)}) %collective-permute-start.10) | collective-permute-done | bytes 327712 | tf_op jit(solution)/shard_map/ppermute | solution.py:22
  147.5 1.9 broadcast.307.clone.2
  151.9 2.1 collective-permute-start.15
  154.0 8.7 %fusion.34 = f32[16,320,128]{2,1,0:T(8,128)} fusion(bf16[16,4096,128]{2,1,0:T(8,128)(2,1)S(1)} %bitcast.213, bf16[320,4096]{1,0:T(8,128)(2,1)} %get-tuple-element.45), kind=kOutput, calls=%fused_computation.42 | convolution fusion | flops 5368709120 | bytes 22020096 | tf_op jit(solution)/shard_map/tf,mfd->mtd/dot_general | solution.py:305
  163.4 4.5 %collective-permute-done.11 = bf16[80,4096]{1,0:T(8,128)(2,1)S(1)} collective-permute-done((bf16[80,4096]{1,0:T(8,128)(2,1)S(1)}, bf16[80,4096]{1,0:T(8,128)(2,1)S(1)}, u32[]{:S(2)}, u32[]{:S(2)}) %collective-permute-start.11) | collective-permute-done | bytes 655392 | tf_op jit(solution)/shard_map/ppermute | solution.py:22
  169.1 1.8 broadcast.307
  170.9 2.3 constant_dynamic-update-slice_fusion.2
  174.9 2.1 collective-permute-start.20
  183.2 2.0 fusion.81
  186.6 3.3 %collective-permute-start.26 = (bf16[16,320,128]{2,1,0:T(8,128)(2,1)}, bf16[16,320,128]{2,1,0:T(8,128)(2,1)}, u32[]{:S(2)}, u32[]{:S(2)}) collective-permute-start(bf16[16,320,128]{2,1,0:T(8,128)(2,1)} %fusion.11), channel_id=1, source_target_pairs={{0,4},{4,0},{1,5},{5,1},{2,6},{6,2},{3,7},{7,3},{8,12},{12,8},{9,1... | collective-permute-start | bytes 3932168 | tf_op jit(solution)/shard_map/ppermute | solution.py:22
  190.1 22.1 %collective-permute-done.13 = bf16[40,4096]{1,0:T(8,128)(2,1)} collective-permute-done((bf16[40,4096]{1,0:T(8,128)(2,1)}, bf16[40,4096]{1,0:T(8,128)(2,1)}, u32[]{:S(2)}, u32[]{:S(2)}) %collective-permute-start.13) | collective-permute-done | bytes 327712 | tf_op jit(solution)/shard_map/ppermute | solution.py:22
  212.2 2.0 maximum_dynamic-update-slice_fusion.2
  214.2 4.7 %fusion.20 = f32[128,2,320]{0,2,1:T(8,128)S(1)} fusion(bf16[320,4096]{1,0:T(8,128)(2,1)} %maximum_dynamic-update-slice_fusion.2, bf16[128,2,4096]{2,1,0:T(2,128)(2,1)S(1)} %copy-done.11), kind=kOutput, calls=%fused_computation.27 | convolution fusion | flops 671088640 | bytes 5046272 | tf_op jit(solution)/shard_map/tf,ckf->ktc/dot_general | solution.py:325
  218.9 4.5 %fusion.59 = f32[2,320,128]{2,1,0:T(8,128)S(1)} fusion(f32[128,2,320]{0,2,1:T(8,128)S(1)} %fusion.20, bf16[320,4096]{1,0:T(8,128)(2,1)} %get-tuple-element.45, bf16[128,2,4096]{2,1,0:T(2,128)(2,1)S(1)} %copy-done.10), kind=kOutput, calls=%fused_computation.51 | convolution fusion | flops 671170560 | bytes 5373952 | tf_op jit(solution)/shard_map/tf,ckf->ktc/dot_general | solution.py:325
  224.9 2.5 collective-permute-start.21
  228.5 2.1 constant_dynamic-update-slice_fusion.1
  230.6 2.0 constant_dynamic-update-slice_fusion
  232.6 13.5 %collective-permute-done.21 = bf16[40,4096]{1,0:T(8,128)(2,1)S(1)} collective-permute-done((bf16[40,4096]{1,0:T(8,128)(2,1)S(1)}, bf16[40,4096]{1,0:T(8,128)(2,1)S(1)}, u32[]{:S(2)}, u32[]{:S(2)}) %collective-permute-start.21) | collective-permute-done | bytes 327712 | tf_op jit(solution)/shard_map/ppermute | solution.py:22
  247.0 4.5 %fusion.14 = f32[128,2,320]{0,2,1:T(8,128)S(1)} fusion(bf16[320,4096]{1,0:T(8,128)(2,1)} %maximum_dynamic-update-slice_fusion.3, bf16[128,2,4096]{2,1,0:T(2,128)(2,1)S(1)} %copy-done.11), kind=kOutput, calls=%fused_computation.21 | convolution fusion | flops 671088640 | bytes 5046272 | tf_op jit(solution)/shard_map/tf,ckf->ktc/dot_general | solution.py:325
  251.5 4.7 %fusion.69 = f32[2,320,128]{2,1,0:T(8,128)S(1)} fusion(f32[128,2,320]{0,2,1:T(8,128)S(1)} %fusion.14, bf16[320,4096]{1,0:T(8,128)(2,1)} %get-tuple-element.46, bf16[128,2,4096]{2,1,0:T(2,128)(2,1)S(1)} %copy-done.10), kind=kOutput, calls=%fused_computation.53 | convolution fusion | flops 671170560 | bytes 5373952 | tf_op jit(solution)/shard_map/tf,ckf->ktc/dot_general | solution.py:325
  256.7 4.2 %collective-permute-start.23 = (bf16[2,480,128]{2,1,0:T(8,128)(2,1)S(1)}, bf16[2,480,128]{2,1,0:T(8,128)(2,1)S(1)}, u32[]{:S(2)}, u32[]{:S(2)}) collective-permute-start(bf16[2,480,128]{2,1,0:T(8,128)(2,1)S(1)} %get-tuple-element.29), channel_id=1, source_target_pairs={{0,0},{1,4},{2,1},{3,5},{4,2},{5,6},{6,3},{7,7},{8,8},{9,12},{10,9... | collective-permute-start | bytes 737288 | tf_op jit(solution)/shard_map/ppermute | solution.py:339
  261.0 3.8 %collective-permute-start.24 = (bf16[2,480,128]{2,1,0:T(8,128)(2,1)S(1)}, bf16[2,480,128]{2,1,0:T(8,128)(2,1)S(1)}, u32[]{:S(2)}, u32[]{:S(2)}) collective-permute-start(bf16[2,480,128]{2,1,0:T(8,128)(2,1)S(1)} %get-tuple-element.30), channel_id=1, source_target_pairs={{0,4},{1,0},{2,5},{3,1},{4,6},{5,2},{6,7},{7,3},{8,12},{9,8},{10,1... | collective-permute-start | bytes 737288 | tf_op jit(solution)/shard_map/ppermute | solution.py:342
  264.7 2.0 fusion.83
  266.7 3.8 %collective-permute-done.23 = bf16[2,480,128]{2,1,0:T(8,128)(2,1)S(1)} collective-permute-done((bf16[2,480,128]{2,1,0:T(8,128)(2,1)S(1)}, bf16[2,480,128]{2,1,0:T(8,128)(2,1)S(1)}, u32[]{:S(2)}, u32[]{:S(2)}) %collective-permute-start.23) | collective-permute-done | bytes 245792 | tf_op jit(solution)/shard_map/ppermute | solution.py:339
  270.5 2.4 collective-permute-done.24
  274.9 5.5 %fusion.138 = (f32[2,2,8,160]{3,2,1,0:T(8,128)S(1)}, f32[2,2,8,160,320]{4,3,2,1,0:T(8,128)}) fusion(pred[2,160,320]{2,1,0:T(8,128)(4,1)S(1)} %copy-done.17, bf16[2,8,2,160,128]{4,3,2,1,0:T(8,128)(2,1)S(1)} %bitcast.205, bf16[2,1,2,320,128]{4,3,1,0,2:T(8,128)(2,1)S(1)} %get-tuple-element.26, bf16[2,1,2,320,128]{4,3,1,0,2:T(8,128)(2,1)S(1)} %get-tuple-element.25), kind=kOutput, calls=%fused_computation.180 | convolution fusion | flops 426148160 | bytes 8642560 | tf_op jit(solution)/shard_map/sub | solution.py:370
  280.4 4.5 %fusion.41 = bf16[2,8,2,160,128]{4,3,1,2,0:T(8,128)(2,1)S(1)} fusion(f32[2,2,8,160,320]{4,3,2,1,0:T(8,128)} %get-tuple-element.42, f32[2,2,8,160]{3,2,1,0:T(8,128)S(1)} %get-tuple-element.41, bf16[2,1,2,320,128]{4,3,1,0,2:T(8,128)(2,1)S(1)} %get-tuple-element.25, bf16[2,1,2,320,128]{4,3,1,0,2:T(8,128)(2,1)S(1)} %get-tuple-element.26), kind=kOutput, calls=%fused_computation.45 | convolution fusion | flops 424017920 | bytes 8540160 | tf_op jit(solution)/shard_map/gbhqk,gbkd->ghbqd/dot_general | solution.py:372
  (160 shorter events, 54.0 us)
Async XLA Ops:
  0.0 7.1 %copy-start.15 = (bf16[48,8192]{1,0:T(8,128)(2,1)S(1)}, bf16[48,8192]{1,0:T(8,128)(2,1)}, u32[]{:S(2)}) copy-start(bf16[48,8192]{1,0:T(8,128)(2,1)} %param.16) | copy-start | bytes 2359300
  1.8 5.5 %copy-start.22 = (s32[2,8]{1,0:T(2,128)S(1)}, s32[2,8]{1,0:T(2,128)}, u32[]{:S(2)}) copy-start(s32[2,8]{1,0:T(2,128)} %param.19) | copy-start | bytes 196
  3.5 39.6 %copy-start.6 = (bf16[80,8192]{1,0:T(8,128)(2,1)}, bf16[80,8192]{1,0:T(8,128)(2,1)S(1)}, u32[]{:S(2)}) copy-start(bf16[80,8192]{1,0:T(8,128)(2,1)S(1)} %fusion.10) | copy-start | bytes 3932164
  4.5 30.8 %collective-permute-start.4 = (bf16[80,4096]{1,0:T(8,128)(2,1)}, bf16[80,4096]{1,0:T(8,128)(2,1)}, u32[]{:S(2)}, u32[]{:S(2)}) collective-permute-start(bf16[80,4096]{1,0:T(8,128)(2,1)} %constant_dynamic-slice_fusion.4), channel_id=1, source_target_pairs={{0,4},{4,0},{1,5},{5,1},{2,6},{6,2},{3,7},{7,3},{8,12},{12,8},{9,1... | collective-permute-start | bytes 1966088 | tf_op jit(solution)/shard_map/ppermute | solution.py:22
  38.3 17.8 %collective-permute-start = (bf16[80,4096]{1,0:T(8,128)(2,1)}, bf16[80,4096]{1,0:T(8,128)(2,1)S(1)}, u32[]{:S(2)}, u32[]{:S(2)}) collective-permute-start(bf16[80,4096]{1,0:T(8,128)(2,1)} %get-tuple-element.20), channel_id=1, source_target_pairs={{0,1},{1,0},{2,3},{3,2},{4,5},{5,4},{6,7},{7,6},{8,9},{9,8},{10,11... | collective-permute-start | bytes 1966088 | tf_op jit(solution)/shard_map/ppermute | solution.py:22
  39.8 35.5 %collective-permute-start.1 = (bf16[80,4096]{1,0:T(8,128)(2,1)}, bf16[80,4096]{1,0:T(8,128)(2,1)}, u32[]{:S(2)}, u32[]{:S(2)}) collective-permute-start(bf16[80,4096]{1,0:T(8,128)(2,1)} %get-tuple-element.20), channel_id=1, source_target_pairs={{0,2},{2,0},{1,3},{3,1},{4,6},{6,4},{5,7},{7,5},{8,10},{10,8},{9,1... | collective-permute-start | bytes 1966088 | tf_op jit(solution)/shard_map/ppermute | solution.py:22
  43.1 14.2 %copy-start.21 = (s32[2,8]{1,0:T(2,128)S(1)}, s32[2,8]{1,0:T(2,128)}, u32[]{:S(2)}) copy-start(s32[2,8]{1,0:T(2,128)} %param.17) | copy-start | bytes 196
  43.1 14.2 %copy-start = (s32[96]{0:T(128)S(1)}, s32[96]{0:T(128)}, u32[]{:S(2)}) copy-start(s32[96]{0:T(128)} %slot.1) | copy-start | bytes 1156
  45.1 33.4 %collective-permute-start.5 = (bf16[80,4096]{1,0:T(8,128)(2,1)}, bf16[80,4096]{1,0:T(8,128)(2,1)}, u32[]{:S(2)}, u32[]{:S(2)}) collective-permute-start(bf16[80,4096]{1,0:T(8,128)(2,1)} %collective-permute-done.4), channel_id=1, source_target_pairs={{0,1},{1,0},{2,3},{3,2},{4,5},{5,4},{6,7},{7,6},{8,9},{9,8},{10,11... | collective-permute-start | bytes 1966088 | tf_op jit(solution)/shard_map/ppermute | solution.py:22
  45.6 40.1 %collective-permute-start.6 = (bf16[80,4096]{1,0:T(8,128)(2,1)}, bf16[80,4096]{1,0:T(8,128)(2,1)S(1)}, u32[]{:S(2)}, u32[]{:S(2)}) collective-permute-start(bf16[80,4096]{1,0:T(8,128)(2,1)} %collective-permute-done.4), channel_id=1, source_target_pairs={{0,2},{2,0},{1,3},{3,1},{4,6},{6,4},{5,7},{7,5},{8,10},{10,8},{9,1... | collective-permute-start | bytes 1966088 | tf_op jit(solution)/shard_map/ppermute | solution.py:22
  57.3 4.6 %copy-start.1 = (bf16[48,1024,128]{2,1,0:T(8,128)(2,1)S(1)}, bf16[48,1024,128]{2,1,0:T(8,128)(2,1)}, u32[]{:S(2)}) copy-start(bf16[48,1024,128]{2,1,0:T(8,128)(2,1)} %refs_0_.1) | copy-start | bytes 37748740
  61.9 2.8 copy-start.2
  64.7 8.4 %copy-start.14 = (bf16[80,4096]{1,0:T(8,128)(2,1)S(1)}, bf16[80,4096]{1,0:T(8,128)(2,1)}, u32[]{:S(2)}) copy-start(bf16[80,4096]{1,0:T(8,128)(2,1)} %copy-done.13) | copy-start | bytes 1966084
  73.1 38.6 %collective-permute-start.9 = (bf16[8,1024,128]{2,1,0:T(8,128)(2,1)}, bf16[8,1024,128]{2,1,0:T(8,128)(2,1)}, u32[]{:S(2)}, u32[]{:S(2)}) collective-permute-start(bf16[8,1024,128]{2,1,0:T(8,128)(2,1)} %get-tuple-element.12), channel_id=1, source_target_pairs={{0,8},{8,0},{1,9},{9,1},{2,10},{10,2},{3,11},{11,3},{4,12},{12,4},... | collective-permute-start | bytes 6291464 | tf_op jit(solution)/shard_map/ppermute | solution.py:203
  73.9 27.2 %collective-permute-start.2 = (bf16[40,4096]{1,0:T(8,128)(2,1)}, bf16[40,4096]{1,0:T(8,128)(2,1)}, u32[]{:S(2)}, u32[]{:S(2)}) collective-permute-start(bf16[40,4096]{1,0:T(8,128)(2,1)} %slice.114), channel_id=1, source_target_pairs={{0,2},{2,0},{1,3},{3,1},{4,6},{6,4},{5,7},{7,5},{8,10},{10,8},{9,1... | collective-permute-start | bytes 983048 | tf_op jit(solution)/shard_map/ppermute | solution.py:22
  77.0 27.4 %collective-permute-start.3 = (bf16[40,4096]{1,0:T(8,128)(2,1)}, bf16[40,4096]{1,0:T(8,128)(2,1)}, u32[]{:S(2)}, u32[]{:S(2)}) collective-permute-start(bf16[40,4096]{1,0:T(8,128)(2,1)} %slice.115), channel_id=1, source_target_pairs={{0,1},{1,0},{2,3},{3,2},{4,5},{5,4},{6,7},{7,6},{8,9},{9,8},{10,11... | collective-permute-start | bytes 983048 | tf_op jit(solution)/shard_map/ppermute | solution.py:22
  80.3 24.2 %collective-permute-start.7 = (bf16[40,4096]{1,0:T(8,128)(2,1)}, bf16[40,4096]{1,0:T(8,128)(2,1)}, u32[]{:S(2)}, u32[]{:S(2)}) collective-permute-start(bf16[40,4096]{1,0:T(8,128)(2,1)} %slice.116), channel_id=1, source_target_pairs={{0,2},{2,0},{1,3},{3,1},{4,6},{6,4},{5,7},{7,5},{8,10},{10,8},{9,1... | collective-permute-start | bytes 983048 | tf_op jit(solution)/shard_map/ppermute | solution.py:22
  85.7 13.2 %collective-permute-start.17 = (bf16[8,64,128]{2,1,0:T(8,128)(2,1)S(1)}, bf16[8,64,128]{2,1,0:T(8,128)(2,1)S(1)}, u32[]{:S(2)}, u32[]{:S(2)}) collective-permute-start(bf16[8,64,128]{2,1,0:T(8,128)(2,1)S(1)} %get-tuple-element.14), channel_id=1, source_target_pairs={{0,8},{8,0},{1,9},{9,1},{2,10},{10,2},{3,11},{11,3},{4,12},{12,4},... | collective-permute-start | bytes 393224 | tf_op jit(solution)/shard_map/ppermute | solution.py:203
  95.2 16.5 %copy-start.4 = (bf16[8,1024,128]{2,1,0:T(8,128)(2,1)S(1)}, bf16[8,1024,128]{2,1,0:T(8,128)(2,1)}, u32[]{:S(2)}) copy-start(bf16[8,1024,128]{2,1,0:T(8,128)(2,1)} %copy-done.3) | copy-start | bytes 6291460
  98.9 10.3 %collective-permute-start.8 = (bf16[40,4096]{1,0:T(8,128)(2,1)}, bf16[40,4096]{1,0:T(8,128)(2,1)}, u32[]{:S(2)}, u32[]{:S(2)}) collective-permute-start(bf16[40,4096]{1,0:T(8,128)(2,1)} %slice.117), channel_id=1, source_target_pairs={{0,1},{1,0},{2,3},{3,2},{4,5},{5,4},{6,7},{7,6},{8,9},{9,8},{10,11... | collective-permute-start | bytes 983048 | tf_op jit(solution)/shard_map/ppermute | solution.py:22
  101.1 68.0 %collective-permute-start.18 = (bf16[80,4096]{1,0:T(8,128)(2,1)}, bf16[80,4096]{1,0:T(8,128)(2,1)}, u32[]{:S(2)}, u32[]{:S(2)}) collective-permute-start(bf16[80,4096]{1,0:T(8,128)(2,1)} %get-tuple-element.19), channel_id=1, source_target_pairs={{0,4},{4,0},{1,5},{5,1},{2,6},{6,2},{3,7},{7,3},{8,12},{12,8},{9,1... | collective-permute-start | bytes 1966088 | tf_op jit(solution)/shard_map/ppermute | solution.py:22
  104.5 78.7 %collective-permute-start.25 = (bf16[8,16,32,128]{3,2,1,0:T(8,128)(2,1)}, bf16[8,16,32,128]{3,2,1,0:T(8,128)(2,1)}, u32[]{:S(2)}, u32[]{:S(2)}) collective-permute-start(bf16[8,16,32,128]{3,2,1,0:T(8,128)(2,1)} %copy-done.5), channel_id=1, source_target_pairs={{0,8},{8,0},{1,9},{9,1},{2,10},{10,2},{3,11},{11,3},{4,12},{12,4},... | collective-permute-start | bytes 3145736 | tf_op jit(solution)/shard_map/ppermute | solution.py:203
  114.9 2.9 %copy-start.20 = (pred[320,8]{0,1:T(8,128)(4,1)S(1)}, pred[320,8]{0,1:T(8,128)(4,1)}, u32[]{:S(2)}) copy-start(pred[320,8]{0,1:T(8,128)(4,1)} %get-tuple-element.36) | copy-start | bytes 7684
  117.7 2.3 copy-start.19
  120.0 34.0 %slice-start = ((s8[16777216]{0:T(1024)(128)(4,1)}), s8[4194304]{0:T(1024)(128)(4,1)S(1)}, s32[]{:S(2)}) async-start(s8[16777216]{0:T(1024)(128)(4,1)} %bitcast.212), calls=%async_computation | async-start | bytes 8388608
  122.4 31.6 %slice-start.1 = ((s8[16777216]{0:T(1024)(128)(4,1)}), s8[4194304]{0:T(1024)(128)(4,1)S(1)}, s32[]{:S(2)}) async-start(s8[16777216]{0:T(1024)(128)(4,1)} %bitcast.212), calls=%async_computation.1 | async-start | bytes 8388608
  122.4 31.6 %slice-start.2 = ((s8[16777216]{0:T(1024)(128)(4,1)}), s8[4194304]{0:T(1024)(128)(4,1)S(1)}, s32[]{:S(2)}) async-start(s8[16777216]{0:T(1024)(128)(4,1)} %bitcast.212), calls=%async_computation.2 | async-start | bytes 8388608
  122.4 31.6 %slice-start.3 = ((s8[16777216]{0:T(1024)(128)(4,1)}), s8[4194304]{0:T(1024)(128)(4,1)S(1)}, s32[]{:S(2)}) async-start(s8[16777216]{0:T(1024)(128)(4,1)} %bitcast.212), calls=%async_computation.3 | async-start | bytes 8388608
  122.5 23.9 %collective-permute-start.10 = (f32[2,320,128]{2,1,0:T(8,128)S(1)}, f32[2,320,128]{2,1,0:T(8,128)S(1)}, u32[]{:S(2)}, u32[]{:S(2)}) collective-permute-start(f32[2,320,128]{2,1,0:T(8,128)S(1)} %pad_maximum_fusion.2), channel_id=1, source_target_pairs={{0,4},{4,0},{1,5},{5,1},{2,6},{6,2},{3,7},{7,3},{8,12},{12,8},{9,1... | collective-permute-start | bytes 983048 | tf_op jit(solution)/shard_map/ppermute | solution.py:22
  137.0 12.3 %copy-start.7 = (bf16[80,8192]{1,0:T(8,128)(2,1)S(1)}, bf16[80,8192]{1,0:T(8,128)(2,1)}, u32[]{:S(2)}) copy-start(bf16[80,8192]{1,0:T(8,128)(2,1)} %copy-done.6) | copy-start | bytes 3932164
  150.3 17.6 %collective-permute-start.11 = (bf16[80,4096]{1,0:T(8,128)(2,1)S(1)}, bf16[80,4096]{1,0:T(8,128)(2,1)S(1)}, u32[]{:S(2)}, u32[]{:S(2)}) collective-permute-start(bf16[80,4096]{1,0:T(8,128)(2,1)S(1)} %get-tuple-element.22), channel_id=1, source_target_pairs={{0,1},{1,0},{2,3},{3,2},{4,5},{5,4},{6,7},{7,6},{8,9},{9,8},{10,11... | collective-permute-start | bytes 1966088 | tf_op jit(solution)/shard_map/ppermute | solution.py:22
  151.9 10.8 %collective-permute-start.15 = (f32[2,320,128]{2,1,0:T(8,128)S(1)}, f32[2,320,128]{2,1,0:T(8,128)S(1)}, u32[]{:S(2)}, u32[]{:S(2)}) collective-permute-start(f32[2,320,128]{2,1,0:T(8,128)S(1)} %maximum_add_fusion), channel_id=1, source_target_pairs={{0,2},{2,0},{1,3},{3,1},{4,6},{6,4},{5,7},{7,5},{8,10},{10,8},{9,1... | collective-permute-start | bytes 983048 | tf_op jit(solution)/shard_map/ppermute | solution.py:22
  162.7 17.7 %collective-permute-start.12 = (bf16[80,4096]{1,0:T(8,128)(2,1)S(1)}, bf16[80,4096]{1,0:T(8,128)(2,1)S(1)}, u32[]{:S(2)}, u32[]{:S(2)}) collective-permute-start(bf16[80,4096]{1,0:T(8,128)(2,1)S(1)} %get-tuple-element.22), channel_id=1, source_target_pairs={{0,2},{2,0},{1,3},{3,1},{4,6},{6,4},{5,7},{7,5},{8,10},{10,8},{9,1... | collective-permute-start | bytes 1966088 | tf_op jit(solution)/shard_map/ppermute | solution.py:22
  162.8 19.4 %collective-permute-start.16 = (f32[2,320,128]{2,1,0:T(8,128)S(1)}, f32[2,320,128]{2,1,0:T(8,128)S(1)}, u32[]{:S(2)}, u32[]{:S(2)}) collective-permute-start(f32[2,320,128]{2,1,0:T(8,128)S(1)} %fusion.157), channel_id=1, source_target_pairs={{0,1},{1,0},{2,3},{3,2},{4,5},{5,4},{6,7},{7,6},{8,9},{9,8},{10,11... | collective-permute-start | bytes 983048 | tf_op jit(solution)/shard_map/ppermute | solution.py:22
  173.2 50.7 %collective-permute-start.19 = (bf16[80,4096]{1,0:T(8,128)(2,1)}, bf16[80,4096]{1,0:T(8,128)(2,1)}, u32[]{:S(2)}, u32[]{:S(2)}) collective-permute-start(bf16[80,4096]{1,0:T(8,128)(2,1)} %get-tuple-element.18), channel_id=1, source_target_pairs={{0,1},{1,0},{2,3},{3,2},{4,5},{5,4},{6,7},{7,6},{8,9},{9,8},{10,11... | collective-permute-start | bytes 1966088 | tf_op jit(solution)/shard_map/ppermute | solution.py:22
  174.9 52.6 %collective-permute-start.20 = (bf16[80,4096]{1,0:T(8,128)(2,1)}, bf16[80,4096]{1,0:T(8,128)(2,1)}, u32[]{:S(2)}, u32[]{:S(2)}) collective-permute-start(bf16[80,4096]{1,0:T(8,128)(2,1)} %get-tuple-element.18), channel_id=1, source_target_pairs={{0,2},{2,0},{1,3},{3,1},{4,6},{6,4},{5,7},{7,5},{8,10},{10,8},{9,1... | collective-permute-start | bytes 1966088 | tf_op jit(solution)/shard_map/ppermute | solution.py:22
  177.7 5.5 %copy-start.18 = (bf16[320,8]{0,1:T(8,128)(2,1)S(1)}, bf16[320,8]{0,1:T(8,128)(2,1)}, u32[]{:S(2)}) copy-start(bf16[320,8]{0,1:T(8,128)(2,1)} %get-tuple-element.35) | copy-start | bytes 15364
  180.3 31.9 %collective-permute-start.13 = (bf16[40,4096]{1,0:T(8,128)(2,1)}, bf16[40,4096]{1,0:T(8,128)(2,1)}, u32[]{:S(2)}, u32[]{:S(2)}) collective-permute-start(bf16[40,4096]{1,0:T(8,128)(2,1)} %slice.120), channel_id=1, source_target_pairs={{0,2},{2,0},{1,3},{3,1},{4,6},{6,4},{5,7},{7,5},{8,10},{10,8},{9,1... | collective-permute-start | bytes 983048 | tf_op jit(solution)/shard_map/ppermute | solution.py:22
  182.1 30.1 %collective-permute-start.14 = (bf16[40,4096]{1,0:T(8,128)(2,1)}, bf16[40,4096]{1,0:T(8,128)(2,1)}, u32[]{:S(2)}, u32[]{:S(2)}) collective-permute-start(bf16[40,4096]{1,0:T(8,128)(2,1)} %slice.121), channel_id=1, source_target_pairs={{0,1},{1,0},{2,3},{3,2},{4,5},{5,4},{6,7},{7,6},{8,9},{9,8},{10,11... | collective-permute-start | bytes 983048 | tf_op jit(solution)/shard_map/ppermute | solution.py:22
  185.3 28.9 %copy-start.11 = (bf16[128,2,4096]{2,1,0:T(2,128)(2,1)S(1)}, bf16[128,2,4096]{2,1,0:T(2,128)(2,1)}, u32[]{:S(2)}) copy-start(bf16[128,2,4096]{2,1,0:T(2,128)(2,1)} %get-tuple-element.24) | copy-start | bytes 6291460
  186.6 86.5 %collective-permute-start.26 = (bf16[16,320,128]{2,1,0:T(8,128)(2,1)}, bf16[16,320,128]{2,1,0:T(8,128)(2,1)}, u32[]{:S(2)}, u32[]{:S(2)}) collective-permute-start(bf16[16,320,128]{2,1,0:T(8,128)(2,1)} %fusion.11), channel_id=1, source_target_pairs={{0,4},{4,0},{1,5},{5,1},{2,6},{6,2},{3,7},{7,3},{8,12},{12,8},{9,1... | collective-permute-start | bytes 3932168 | tf_op jit(solution)/shard_map/ppermute | solution.py:22
  214.2 4.7 %copy-start.10 = (bf16[128,2,4096]{2,1,0:T(2,128)(2,1)S(1)}, bf16[128,2,4096]{2,1,0:T(2,128)(2,1)}, u32[]{:S(2)}) copy-start(bf16[128,2,4096]{2,1,0:T(2,128)(2,1)} %get-tuple-element.23) | copy-start | bytes 6291460
  218.9 4.5 %copy-start.16 = (bf16[8,128,64]{2,1,0:T(8,128)(2,1)S(1)}, bf16[8,128,64]{2,1,0:T(8,128)(2,1)}, u32[]{:S(2)}) copy-start(bf16[8,128,64]{2,1,0:T(8,128)(2,1)} %reshape.435) | copy-start | bytes 393220
  224.9 21.2 %collective-permute-start.21 = (bf16[40,4096]{1,0:T(8,128)(2,1)S(1)}, bf16[40,4096]{1,0:T(8,128)(2,1)S(1)}, u32[]{:S(2)}, u32[]{:S(2)}) collective-permute-start(bf16[40,4096]{1,0:T(8,128)(2,1)S(1)} %slice.127), channel_id=1, source_target_pairs={{0,2},{2,0},{1,3},{3,1},{4,6},{6,4},{5,7},{7,5},{8,10},{10,8},{9,1... | collective-permute-start | bytes 983048 | tf_op jit(solution)/shard_map/ppermute | solution.py:22
  228.5 17.6 %collective-permute-start.22 = (bf16[40,4096]{1,0:T(8,128)(2,1)S(1)}, bf16[40,4096]{1,0:T(8,128)(2,1)S(1)}, u32[]{:S(2)}, u32[]{:S(2)}) collective-permute-start(bf16[40,4096]{1,0:T(8,128)(2,1)S(1)} %slice.128), channel_id=1, source_target_pairs={{0,1},{1,0},{2,3},{3,2},{4,5},{5,4},{6,7},{7,6},{8,9},{9,8},{10,11... | collective-permute-start | bytes 983048 | tf_op jit(solution)/shard_map/ppermute | solution.py:22
  256.7 13.8 %collective-permute-start.23 = (bf16[2,480,128]{2,1,0:T(8,128)(2,1)S(1)}, bf16[2,480,128]{2,1,0:T(8,128)(2,1)S(1)}, u32[]{:S(2)}, u32[]{:S(2)}) collective-permute-start(bf16[2,480,128]{2,1,0:T(8,128)(2,1)S(1)} %get-tuple-element.29), channel_id=1, source_target_pairs={{0,0},{1,4},{2,1},{3,5},{4,2},{5,6},{6,3},{7,7},{8,8},{9,12},{10,9... | collective-permute-start | bytes 737288 | tf_op jit(solution)/shard_map/ppermute | solution.py:339
  261.0 12.0 %collective-permute-start.24 = (bf16[2,480,128]{2,1,0:T(8,128)(2,1)S(1)}, bf16[2,480,128]{2,1,0:T(8,128)(2,1)S(1)}, u32[]{:S(2)}, u32[]{:S(2)}) collective-permute-start(bf16[2,480,128]{2,1,0:T(8,128)(2,1)S(1)} %get-tuple-element.30), channel_id=1, source_target_pairs={{0,4},{1,0},{2,5},{3,1},{4,6},{5,2},{6,7},{7,3},{8,12},{9,8},{10,1... | collective-permute-start | bytes 737288 | tf_op jit(solution)/shard_map/ppermute | solution.py:342
  264.7 8.4 %copy-start.9 = (f32[16,320,128]{2,1,0:T(8,128)S(1)}, f32[16,320,128]{2,1,0:T(8,128)}, u32[]{:S(2)}) copy-start(f32[16,320,128]{2,1,0:T(8,128)} %fusion.34) | copy-start | bytes 7864324
  (6 other events, 8.5 us)
where the time goes:
time: 287 us; the launch traced here: 286 us
  waiting for transfers between devices  94.3 us (33%)
  local copies, waits for them, and re-layouts  61.9 us (22%)
  matrix products  57.5 us (20%)
  starting transfers between devices  39.9 us (14%)
  other arithmetic  23.2 us (8%)
  Pallas kernels  6.1 us (2%)
  between operations  3.26 us (1%)
    ppermute x22, waiting for transfers between devices, partner_2(): return lax.ppermute(block, axis, route)  88 us
    ppermute x22, starting transfers between devices, partner_2(): return lax.ppermute(block, axis, route)  31.9 us
    dot_general x2, matrix products, query_base(): jnp.einsum('tf,mfd->mtd', gathered, query_weight, preferred_element_type=...  19.8 us
    dynamic_update_slice x10, local copies, waits for them, and re-layouts, side_gather(): lax.dynamic_update_slice_in_dim(result, piece, (index ^ mask) * count, 0)  15.7 us
    unnamed x55, local copies, waits for them, and re-layouts  10.1 us
    dot_general x2, matrix products, key_values(): jnp.einsum('tf,ckf->ktc', near, kv_near, preferred_element_type=f32)  9.22 us
    dot_general x2, matrix products, key_values(): jnp.einsum('tf,ckf->ktc', far, kv_far, preferred_element_type=f32)  9.18 us
    dynamic_update_slice x5, other arithmetic, side_gather(): lax.dynamic_update_slice_in_dim(result, piece, (index ^ mask) * count, 0)  8.58 us
  transfers between devices with their start and end apart: 27, of which 10 were waited for; matrix products, arithmetic and copies ran while one was open for 39% of the time, Pallas kernels for 2%

commit v1 on v0

--- a/solution.py
+++ b/solution.py
@@ -203,7 +203,7 @@
         received = lax.ppermute(theirs, "replica", [(0, 1), (1, 0)])
         keep = here.reshape((count,) + (1,) * (own.ndim - 1))
         result.append(jnp.where(keep, own, received))
-    return result
+    return result, picked[0][0]
 
 
 def on_square(
@@ -243,10 +243,8 @@
     other_near = swap(far_half, 2)
     own_near_all, first_in = side_gather(near_half, index)
     zero = (first_in[0, 0] * jnp.zeros((), bf)).astype(jnp.int32)
-    other_near_all, _ = side_gather(other_near, index)
-    other_far = swap(after(near_half, other_near), 2)
-
-    down_sel, upq_sel, upv_sel = fetch_adapters(
+
+    (down_sel, upq_sel, upv_sel), picked = fetch_adapters(
         (
             adapter_down_weight,
             adapter_up_query,
@@ -256,6 +254,8 @@
         adapter_slot,
         replica_now,
     )
+    other_near_all, _ = side_gather(after(other_near, picked), index)
+    other_far = swap(after(near_half, other_near), 2)
     requests = down_sel.shape[0]
 
     lengths_mine = lax.dynamic_index_in_dim(request_row_lengths, replica_now, 0, keepdims=False)
@@ -283,7 +283,7 @@
     down_other = down_part(other_near_all, other_member)
     crossed = swap(jnp.stack([down_other, down_own], axis=0), 2)
     down = jnp.stack([down_own, down_other], axis=0) + crossed
-    own_far_all, last = side_gather(after(far_half, crossed[0].astype(bf)), index)
+    own_far_all, last = side_gather(after(far_half, down_other.astype(bf)), index)
     other_far_all, _ = side_gather(after(other_far, last), index)
     down = down + swap(down, 1)
     down = (down + swap(down, 0)).astype(bf)
@@ -311,12 +311,14 @@
             "tj,mjd->mtd", expand(member, ranks), upq_mat, preferred_element_type=f32
         )
 
-    received = swap(query_part(query_base(other_near_all), other_member, down[1]).astype(bf), 2)
+    send = query_part(query_base(other_near_all), other_member, down[1]).astype(bf)
+    received = swap(send, 2)
+    later = (send[0, 0, 0] * jnp.zeros((), bf)).astype(jnp.int32)
     own_query = query_part(query_base(own_near_all), own_member, down[0])
     query = (own_query + received.astype(f32)).astype(bf)
 
-    kv_near = lax.dynamic_slice_in_dim(key_value_weight, (side + zero) * half_width, half_width, 2)
-    kv_far = lax.dynamic_slice_in_dim(key_value_weight, (1 - side + zero) * half_width, half_width, 2)
+    kv_near = lax.dynamic_slice_in_dim(key_value_weight, (side + later) * half_width, half_width, 2)
+    kv_far = lax.dynamic_slice_in_dim(key_value_weight, (1 - side + later) * half_width, half_width, 2)
     upv_mat = jnp.transpose(
         upv_sel.reshape(requests, HEAD_WIDTH, rank), (0, 2, 1)
     ).reshape(requests * rank, HEAD_WIDTH)

time: 287 us -> 276 us (0.962)
  waiting for transfers between devices: 94.3 us -> 74 us
  starting transfers between devices: 39.9 us -> 55.7 us
  local copies, waits for them, and re-layouts: 61.9 us -> 52.6 us
    ppermute x1, starting transfers between devices: 3.76 us -> 25.2 us  [on_square(): lax.ppermute(jnp.where(odd, for_low, for_high), 'tensor', [(c, c // 2 + 4...]
    ppermute x22, waiting for transfers between devices: 88 us -> 70.4 us  [partner_2(): return lax.ppermute(block, axis, route)]
    dynamic_update_slice x10 -> x9, local copies, waits for them, and re-layouts: 15.7 us -> 11.3 us  [side_gather(): lax.dynamic_update_slice_in_dim(result, piece, (index ^ mask) * count, 0)]
    ppermute x1, waiting for transfers between devices: 3.83 us -> 0.01 us  [on_square(): lax.ppermute(jnp.where(odd, for_high, for_low), 'tensor', [(c, c // 2 + 4...]
    ppermute x22, starting transfers between devices: 31.9 us -> 28.5 us  [partner_2(): return lax.ppermute(block, axis, route)]
    another operation x4, local copies, waits for them, and re-layouts: 7.37 us -> 4.24 us
    unnamed x55 -> x63, local copies, waits for them, and re-layouts: 10.1 us -> 11.6 us
    dynamic_update_slice x5 -> x7, other arithmetic: 8.58 us -> 8.09 us  [side_gather(): lax.dynamic_update_slice_in_dim(result, piece, (index ^ mask) * count, 0)]
  transfers between devices with their start and end apart: 27 -> 27, of which waited for: 10 -> 12; matrix products, arithmetic and copies ran while one was open for 39% -> 37% of each run, Pallas kernels for 2% -> 2%
where the time goes in v1:
time: 276 us; the launch traced here: 273 us
  waiting for transfers between devices  74 us (27%)
  starting transfers between devices  55.7 us (20%)
  matrix products  54.9 us (20%)
  local copies, waits for them, and re-layouts  52.6 us (19%)
  other arithmetic  25.2 us (9%)
  Pallas kernels  5.94 us (2%)
  between operations  4.88 us (2%)
    ppermute x22, waiting for transfers between devices, partner_2(): return lax.ppermute(block, axis, route)  70.4 us
    ppermute x22, starting transfers between devices, partner_2(): return lax.ppermute(block, axis, route)  28.5 us
    ppermute x1, starting transfers between devices, on_square(): lax.ppermute(jnp.where(odd, for_low, for_high), 'tensor', [(c, c // 2 + 4...  25.2 us
    dot_general x2, matrix products, query_base(): jnp.einsum('tf,mfd->mtd', gathered, query_weight, preferred_element_type=...  21.9 us
    unnamed x63, local copies, waits for them, and re-layouts  11.6 us
    dynamic_update_slice x9, local copies, waits for them, and re-layouts, side_gather(): lax.dynamic_update_slice_in_dim(result, piece, (index ^ mask) * count, 0)  11.3 us
    dot_general x2, matrix products, key_values(): jnp.einsum('tf,ckf->ktc', far, kv_far, preferred_element_type=f32)  8.7 us
    dynamic_update_slice x7, other arithmetic, side_gather(): lax.dynamic_update_slice_in_dim(result, piece, (index ^ mask) * count, 0)  8.09 us
  transfers between devices with their start and end apart: 27, of which 12 were waited for; matrix products, arithmetic and copies ran while one was open for 37% of the time, Pallas kernels for 2%

profile of v1, /device:TPU:12, one launch (start us, length us, event | category | flops | bytes accessed | tf_op | source)
XLA Modules:
  0.0 273.1 jit_solution(3595294635803378132)
XLA Ops:
  0.0 1.7 fusion.8
  1.8 1.7 fusion.10
  4.5 2.6 collective-permute-start
  11.6 23.7 %collective-permute-done = bf16[80,4096]{1,0:T(8,128)(2,1)S(1)} collective-permute-done((bf16[80,4096]{1,0:T(8,128)(2,1)}, bf16[80,4096]{1,0:T(8,128)(2,1)S(1)}, u32[]{:S(2)}, u32[]{:S(2)}) %collective-permute-start) | collective-permute-done | bytes 655392 | tf_op jit(solution)/shard_map/ppermute | solution.py:22
  42.0 2.0 collective-permute-start.19
  47.0 7.8 %collective-permute-done.1 = bf16[80,4096]{1,0:T(8,128)(2,1)S(1)} collective-permute-done((bf16[80,4096]{1,0:T(8,128)(2,1)}, bf16[80,4096]{1,0:T(8,128)(2,1)S(1)}, u32[]{:S(2)}, u32[]{:S(2)}) %collective-permute-start.1) | collective-permute-done | bytes 655392 | tf_op jit(solution)/shard_map/ppermute | solution.py:22
  56.1 4.6 %copy-done.1 = bf16[48,1024,128]{2,1,0:T(8,128)(2,1)S(1)} copy-done((bf16[48,1024,128]{2,1,0:T(8,128)(2,1)S(1)}, bf16[48,1024,128]{2,1,0:T(8,128)(2,1)}, u32[]{:S(2)}) %copy-start.1) | copy-done | bytes 12582936
  60.7 2.8 %copy-done.2 = bf16[48,16,32,128]{3,2,1,0:T(8,128)(2,1)S(1)} copy-done((bf16[48,16,32,128]{3,2,1,0:T(8,128)(2,1)S(1)}, bf16[48,16,32,128]{3,2,1,0:T(8,128)(2,1)}, u32[]{:S(2)}) %copy-start.2) | copy-done | bytes 6291480
  63.5 5.9 %shard_map.100 = (bf16[8,1024,128]{2,1,0:T(8,128)(2,1)}, bf16[8,16,32,128]{3,2,1,0:T(8,128)(2,1)S(1)}, bf16[8,64,128]{2,1,0:T(8,128)(2,1)S(1)}, bf16[8,1024,128]...) custom-call(s32[2,8]{1,0:T(2,128)S(1)} %broadcast_add_fusion.4.wanted, ...), custom_call_target="tpu_custom_call" | custom-call | tf_op jit(solution)/shard_map/pallas_call | solution.py:190
  71.8 1.7 slice.125
  78.9 2.0 constant_dynamic-update-slice_fusion.6
  80.9 1.8 broadcast.307.clone.1
  85.6 1.8 collective-permute-start.3
  87.4 2.0 maximum_dynamic-update-slice_fusion.1
  89.4 11.0 %fusion.37 = f32[16,320,128]{2,1,0:T(8,128)} fusion(bf16[16,4096,128]{2,1,0:T(8,128)(2,1)} %param.12, bf16[320,4096]{1,0:T(8,128)(2,1)} %maximum_dynamic-update-slice_fusion.1), kind=kOutput, calls=%fused_computation.43 | convolution fusion | flops 5368709120 | bytes 22020096 | tf_op jit(solution)/shard_map/tf,mfd->mtd/dot_general | solution.py:305
  100.4 2.4 collective-permute-done.3
  105.3 1.8 collective-permute-start.4
  107.1 2.0 constant_dynamic-update-slice_fusion.10
  110.0 1.9 collective-permute-done.5
  111.9 2.2 collective-permute-done.4
  115.0 3.2 %select_bitcast_fusion = bf16[1024,8,128]{2,0,1:T(8,128)(2,1)} fusion(bf16[8,1024,128]{2,1,0:T(8,128)(2,1)S(1)} %copy-done.4, bf16[8,1024,128]{2,1,0:T(8,128)(2,1)} %collective-permute-done.10, pred[8]{0:T(512)(128)(4,1)S(1)} %compare_and_fusion.3), kind=kLoop, calls=%fused_computation.37 | loop fusion | flops 1048576 | bytes 6291464 | tf_op jit(solution)/shard_map/transpose | solution.py:273
  118.2 3.9 %copy.36 = bf16[1024,8,128]{0,2,1:T(8,128)(2,1)} copy(bf16[1024,8,128]{2,0,1:T(8,128)(2,1)} %select_bitcast_fusion) | data formatting | bytes 4194304 | tf_op jit(solution)/shard_map/transpose | solution.py:273
  122.1 2.8 %fusion.48 = f32[320,128]{1,0:T(8,128)S(1)} fusion(bf16[1024,8,128]{0,2,1:T(8,128)(2,1)} %copy.36, bf16[320,4096]{1,0:T(8,128)(2,1)} %maximum_dynamic-update-slice_fusion, s32[]{:T(128)S(6)} %select_n.167, pred[320,8]{0,1:T(8,128)(4,1)S(1)} %copy-done.28), kind=kOutput, calls=%fused_computation.48 | convolution fusion | flops 671703040 | bytes 2918916 | tf_op jit(solution)/shard_map/dot_general | solution.py:277
  126.1 1.8 broadcast.307.clone.2
  129.5 1.7 collective-permute-start.15
  131.2 2.2 fusion.51
  133.5 3.3 %collective-permute-start.11 = (f32[2,320,128]{2,1,0:T(8,128)S(1)}, f32[2,320,128]{2,1,0:T(8,128)S(1)}, u32[]{:S(2)}, u32[]{:S(2)}) collective-permute-start(f32[2,320,128]{2,1,0:T(8,128)S(1)} %pad_maximum_fusion.2), channel_id=1, source_target_pairs={{0,4},{4,0},{1,5},{5,1},{2,6},{6,2},{3,7},{7,3},{8,12},{12,8},{9,1... | collective-permute-start | bytes 983048 | tf_op jit(solution)/shard_map/ppermute | solution.py:22
  136.8 10.9 %fusion.34 = f32[16,320,128]{2,1,0:T(8,128)} fusion(bf16[16,4096,128]{2,1,0:T(8,128)(2,1)} %param.12, bf16[320,4096]{1,0:T(8,128)(2,1)} %maximum_dynamic-update-slice_fusion), kind=kOutput, calls=%fused_computation.42 | convolution fusion | flops 5368709120 | bytes 22020096 | tf_op jit(solution)/shard_map/tf,mfd->mtd/dot_general | solution.py:305
  147.7 8.4 %collective-permute-done.11 = f32[2,320,128]{2,1,0:T(8,128)S(1)} collective-permute-done((f32[2,320,128]{2,1,0:T(8,128)S(1)}, f32[2,320,128]{2,1,0:T(8,128)S(1)}, u32[]{:S(2)}, u32[]{:S(2)}) %collective-permute-start.11) | collective-permute-done | bytes 327712 | tf_op jit(solution)/shard_map/ppermute | solution.py:22
  156.3 1.7 collective-permute-start.17
  158.0 2.1 collective-permute-start.16
  161.6 2.1 constant_dynamic-update-slice_fusion.2
  166.7 1.9 collective-permute-start.13
  168.5 4.2 %collective-permute-done.16 = bf16[40,4096]{1,0:T(8,128)(2,1)S(1)} collective-permute-done((bf16[40,4096]{1,0:T(8,128)(2,1)S(1)}, bf16[40,4096]{1,0:T(8,128)(2,1)S(1)}, u32[]{:S(2)}, u32[]{:S(2)}) %collective-permute-start.16) | collective-permute-done | bytes 327712 | tf_op jit(solution)/shard_map/ppermute | solution.py:22
  173.6 10.9 %collective-permute-done.13 = f32[2,320,128]{2,1,0:T(8,128)S(1)} collective-permute-done((f32[2,320,128]{2,1,0:T(8,128)S(1)}, f32[2,320,128]{2,1,0:T(8,128)S(1)}, u32[]{:S(2)}, u32[]{:S(2)}) %collective-permute-start.13) | collective-permute-done | bytes 327712 | tf_op jit(solution)/shard_map/ppermute | solution.py:22
  190.0 6.4 %constant_dynamic-slice_fusion.2 = (bf16[128,2,4096]{2,1,0:T(2,128)(2,1)S(1)}, bf16[128,2,4096]{2,1,0:T(2,128)(2,1)S(1)}) fusion(bf16[128,2,8192]{2,1,0:T(2,128)(2,1)} %param.13, s32[]{:T(128)S(6)} %select_n.172, s32[]{:T(128)S(6)} %select_n.173), kind=kLoop, calls=%fused_computation.140 | loop fusion | bytes 8388616 | tf_op jit(solution)/shard_map/dynamic_slice | solution.py:320
  196.4 6.0 %fusion.16 = f32[128,2,320]{0,2,1:T(8,128)S(1)} fusion(bf16[320,4096]{1,0:T(8,128)(2,1)} %maximum_dynamic-update-slice_fusion.2, bf16[128,2,4096]{2,1,0:T(2,128)(2,1)S(1)} %get-tuple-element.26), kind=kOutput, calls=%fused_computation.23 | convolution fusion | flops 671088640 | bytes 5046272 | tf_op jit(solution)/shard_map/tf,ckf->ktc/dot_general | solution.py:327
  202.5 2.9 %fusion.69 = f32[2,320,128]{2,1,0:T(8,128)S(1)} fusion(f32[128,2,320]{0,2,1:T(8,128)S(1)} %fusion.16, bf16[320,4096]{1,0:T(8,128)(2,1)S(1)} %copy-done.11, bf16[128,2,4096]{2,1,0:T(2,128)(2,1)S(1)} %get-tuple-element.25), kind=kOutput, calls=%fused_computation.53 | convolution fusion | flops 671170560 | bytes 5373952 | tf_op jit(solution)/shard_map/tf,ckf->ktc/dot_general | solution.py:327
  212.5 1.9 collective-permute-done.23
  214.4 6.6 %collective-permute-done.22 = bf16[40,4096]{1,0:T(8,128)(2,1)S(1)} collective-permute-done((bf16[40,4096]{1,0:T(8,128)(2,1)S(1)}, bf16[40,4096]{1,0:T(8,128)(2,1)S(1)}, u32[]{:S(2)}, u32[]{:S(2)}) %collective-permute-start.22) | collective-permute-done | bytes 327712 | tf_op jit(solution)/shard_map/ppermute | solution.py:22
  221.1 2.7 fusion.14
  223.8 4.5 %fusion.59 = f32[2,320,128]{2,1,0:T(8,128)S(1)} fusion(f32[128,2,320]{0,2,1:T(8,128)S(1)} %fusion.14, bf16[320,4096]{1,0:T(8,128)(2,1)} %maximum_dynamic-update-slice_fusion, bf16[128,2,4096]{2,1,0:T(2,128)(2,1)S(1)} %copy-done.14), kind=kOutput, calls=%fused_computation.51 | convolution fusion | flops 671170560 | bytes 5373952 | tf_op jit(solution)/shard_map/tf,ckf->ktc/dot_general | solution.py:327
  228.7 1.9 collective-permute-start.24
  230.7 25.2 %collective-permute-start.25 = (bf16[2,480,128]{2,1,0:T(8,128)(2,1)S(1)}, bf16[2,480,128]{2,1,0:T(8,128)(2,1)S(1)}, u32[]{:S(2)}, u32[]{:S(2)}) collective-permute-start(bf16[2,480,128]{2,1,0:T(8,128)(2,1)S(1)} %get-tuple-element.32), channel_id=1, source_target_pairs={{0,4},{1,0},{2,5},{3,1},{4,6},{5,2},{6,7},{7,3},{8,12},{9,8},{10,1... | collective-permute-start | bytes 737288 | tf_op jit(solution)/shard_map/ppermute | solution.py:344
  256.4 3.6 %collective-permute-done.25 = bf16[2,480,128]{2,1,0:T(8,128)(2,1)S(1)} collective-permute-done((bf16[2,480,128]{2,1,0:T(8,128)(2,1)S(1)}, bf16[2,480,128]{2,1,0:T(8,128)(2,1)S(1)}, u32[]{:S(2)}, u32[]{:S(2)}) %collective-permute-start.25) | collective-permute-done | bytes 245792 | tf_op jit(solution)/shard_map/ppermute | solution.py:344
  260.2 1.8 fusion.12
  261.9 5.5 %fusion.137 = (f32[2,2,8,160]{3,2,1,0:T(8,128)S(1)}, f32[2,2,8,160,320]{4,3,2,1,0:T(8,128)}) fusion(pred[2,160,320]{2,1,0:T(8,128)(4,1)S(1)} %copy-done.25, bf16[2,8,2,160,128]{4,3,2,1,0:T(8,128)(2,1)S(1)} %bitcast.208, bf16[2,1,2,320,128]{4,3,1,0,2:T(8,128)(2,1)S(1)} %get-tuple-element.28, bf16[2,1,2,320,128]{4,3,1,0,2:T(8,128)(2,1)S(1)} %get-tuple-element.27), kind=kOutput, calls=%fused_computation.180 | convolution fusion | flops 426148160 | bytes 8642560 | tf_op jit(solution)/shard_map/sub | solution.py:372
  267.4 4.5 %fusion.41 = bf16[2,8,2,160,128]{4,3,1,2,0:T(8,128)(2,1)S(1)} fusion(f32[2,2,8,160,320]{4,3,2,1,0:T(8,128)} %get-tuple-element.44, f32[2,2,8,160]{3,2,1,0:T(8,128)S(1)} %get-tuple-element.43, bf16[2,1,2,320,128]{4,3,1,0,2:T(8,128)(2,1)S(1)} %get-tuple-element.27, bf16[2,1,2,320,128]{4,3,1,0,2:T(8,128)(2,1)S(1)} %get-tuple-element.28), kind=kOutput, calls=%fused_computation.45 | convolution fusion | flops 424017920 | bytes 8540160 | tf_op jit(solution)/shard_map/gbhqk,gbkd->ghbqd/dot_general | solution.py:374
  (169 shorter events, 50.5 us)
Async XLA Ops:
  0.0 7.7 %copy-start.30 = (s32[2,8]{1,0:T(2,128)S(1)}, s32[2,8]{1,0:T(2,128)}, u32[]{:S(2)}) copy-start(s32[2,8]{1,0:T(2,128)} %param.19) | copy-start | bytes 196
  0.0 8.4 %copy-start.21 = (bf16[48,8192]{1,0:T(8,128)(2,1)S(1)}, bf16[48,8192]{1,0:T(8,128)(2,1)}, u32[]{:S(2)}) copy-start(bf16[48,8192]{1,0:T(8,128)(2,1)} %param.16) | copy-start | bytes 2359300
  3.5 40.9 %copy-start.5 = (bf16[80,8192]{1,0:T(8,128)(2,1)}, bf16[80,8192]{1,0:T(8,128)(2,1)S(1)}, u32[]{:S(2)}) copy-start(bf16[80,8192]{1,0:T(8,128)(2,1)S(1)} %fusion.10) | copy-start | bytes 3932164
  4.5 30.8 %collective-permute-start = (bf16[80,4096]{1,0:T(8,128)(2,1)}, bf16[80,4096]{1,0:T(8,128)(2,1)S(1)}, u32[]{:S(2)}, u32[]{:S(2)}) collective-permute-start(bf16[80,4096]{1,0:T(8,128)(2,1)} %constant_dynamic-slice_fusion.7), channel_id=1, source_target_pairs={{0,4},{4,0},{1,5},{5,1},{2,6},{6,2},{3,7},{7,3},{8,12},{12,8},{9,1... | collective-permute-start | bytes 1966088 | tf_op jit(solution)/shard_map/ppermute | solution.py:22
  36.6 19.5 %copy-start.29 = (s32[2,8]{1,0:T(2,128)S(1)}, s32[2,8]{1,0:T(2,128)}, u32[]{:S(2)}) copy-start(s32[2,8]{1,0:T(2,128)} %param.17) | copy-start | bytes 196
  36.6 19.5 %copy-start = (s32[96]{0:T(128)S(1)}, s32[96]{0:T(128)}, u32[]{:S(2)}) copy-start(s32[96]{0:T(128)} %slot.1) | copy-start | bytes 1156
  37.9 16.9 %collective-permute-start.1 = (bf16[80,4096]{1,0:T(8,128)(2,1)}, bf16[80,4096]{1,0:T(8,128)(2,1)S(1)}, u32[]{:S(2)}, u32[]{:S(2)}) collective-permute-start(bf16[80,4096]{1,0:T(8,128)(2,1)} %get-tuple-element.20), channel_id=1, source_target_pairs={{0,1},{1,0},{2,3},{3,2},{4,5},{5,4},{6,7},{7,6},{8,9},{9,8},{10,11... | collective-permute-start | bytes 1966088 | tf_op jit(solution)/shard_map/ppermute | solution.py:22
  40.8 31.1 %collective-permute-start.7 = (bf16[80,4096]{1,0:T(8,128)(2,1)}, bf16[80,4096]{1,0:T(8,128)(2,1)}, u32[]{:S(2)}, u32[]{:S(2)}) collective-permute-start(bf16[80,4096]{1,0:T(8,128)(2,1)} %get-tuple-element.20), channel_id=1, source_target_pairs={{0,2},{2,0},{1,3},{3,1},{4,6},{6,4},{5,7},{7,5},{8,10},{10,8},{9,1... | collective-permute-start | bytes 1966088 | tf_op jit(solution)/shard_map/ppermute | solution.py:22
  42.0 119.2 %collective-permute-start.19 = (bf16[80,4096]{1,0:T(8,128)(2,1)}, bf16[80,4096]{1,0:T(8,128)(2,1)}, u32[]{:S(2)}, u32[]{:S(2)}) collective-permute-start(bf16[80,4096]{1,0:T(8,128)(2,1)} %get-tuple-element.19), channel_id=1, source_target_pairs={{0,4},{4,0},{1,5},{5,1},{2,6},{6,2},{3,7},{7,3},{8,12},{12,8},{9,1... | collective-permute-start | bytes 1966088 | tf_op jit(solution)/shard_map/ppermute | solution.py:22
  56.1 4.6 %copy-start.1 = (bf16[48,1024,128]{2,1,0:T(8,128)(2,1)S(1)}, bf16[48,1024,128]{2,1,0:T(8,128)(2,1)}, u32[]{:S(2)}) copy-start(bf16[48,1024,128]{2,1,0:T(8,128)(2,1)} %refs_0_.1) | copy-start | bytes 37748740
  63.5 11.6 %copy-start.19 = (bf16[80,4096]{1,0:T(8,128)(2,1)S(1)}, bf16[80,4096]{1,0:T(8,128)(2,1)}, u32[]{:S(2)}) copy-start(bf16[80,4096]{1,0:T(8,128)(2,1)} %copy-done.18) | copy-start | bytes 1966084
  70.8 7.3 %copy-start.20 = (bf16[80,4096]{1,0:T(8,128)(2,1)S(1)}, bf16[80,4096]{1,0:T(8,128)(2,1)}, u32[]{:S(2)}) copy-start(bf16[80,4096]{1,0:T(8,128)(2,1)} %copy-done.18) | copy-start | bytes 1966084
  70.8 44.2 %collective-permute-start.10 = (bf16[8,1024,128]{2,1,0:T(8,128)(2,1)}, bf16[8,1024,128]{2,1,0:T(8,128)(2,1)}, u32[]{:S(2)}, u32[]{:S(2)}) collective-permute-start(bf16[8,1024,128]{2,1,0:T(8,128)(2,1)} %get-tuple-element.11), channel_id=1, source_target_pairs={{0,8},{8,0},{1,9},{9,1},{2,10},{10,2},{3,11},{11,3},{4,12},{12,4},... | collective-permute-start | bytes 6291464 | tf_op jit(solution)/shard_map/ppermute | solution.py:203
  73.6 12.1 %collective-permute-start.9 = (bf16[40,4096]{1,0:T(8,128)(2,1)}, bf16[40,4096]{1,0:T(8,128)(2,1)}, u32[]{:S(2)}, u32[]{:S(2)}) collective-permute-start(bf16[40,4096]{1,0:T(8,128)(2,1)} %slice.125), channel_id=1, source_target_pairs={{0,1},{1,0},{2,3},{3,2},{4,5},{5,4},{6,7},{7,6},{8,9},{9,8},{10,11... | collective-permute-start | bytes 983048 | tf_op jit(solution)/shard_map/ppermute | solution.py:22
  75.8 11.6 %collective-permute-start.8 = (bf16[40,4096]{1,0:T(8,128)(2,1)}, bf16[40,4096]{1,0:T(8,128)(2,1)}, u32[]{:S(2)}, u32[]{:S(2)}) collective-permute-start(bf16[40,4096]{1,0:T(8,128)(2,1)} %slice.124), channel_id=1, source_target_pairs={{0,2},{2,0},{1,3},{3,1},{4,6},{6,4},{5,7},{7,5},{8,10},{10,8},{9,1... | collective-permute-start | bytes 983048 | tf_op jit(solution)/shard_map/ppermute | solution.py:22
  77.9 4.8 %copy-start.23 = (bf16[80,4096]{1,0:T(8,128)(2,1)S(1)}, bf16[80,4096]{1,0:T(8,128)(2,1)}, u32[]{:S(2)}) copy-start(bf16[80,4096]{1,0:T(8,128)(2,1)} %copy-done.22) | copy-start | bytes 1966084
  78.0 6.2 %collective-permute-start.18 = (bf16[8,64,128]{2,1,0:T(8,128)(2,1)S(1)}, bf16[8,64,128]{2,1,0:T(8,128)(2,1)S(1)}, u32[]{:S(2)}, u32[]{:S(2)}) collective-permute-start(bf16[8,64,128]{2,1,0:T(8,128)(2,1)S(1)} %get-tuple-element.16), channel_id=1, source_target_pairs={{0,8},{8,0},{1,9},{9,1},{2,10},{10,2},{3,11},{11,3},{4,12},{12,4},... | collective-permute-start | bytes 393224 | tf_op jit(solution)/shard_map/ppermute | solution.py:203
  84.1 20.2 %collective-permute-start.2 = (bf16[80,4096]{1,0:T(8,128)(2,1)}, bf16[80,4096]{1,0:T(8,128)(2,1)}, u32[]{:S(2)}, u32[]{:S(2)}) collective-permute-start(bf16[80,4096]{1,0:T(8,128)(2,1)} %get-tuple-element.24), channel_id=1, source_target_pairs={{0,1},{1,0},{2,3},{3,2},{4,5},{5,4},{6,7},{7,6},{8,9},{9,8},{10,11... | collective-permute-start | bytes 1966088 | tf_op jit(solution)/shard_map/ppermute | solution.py:22
  85.6 17.1 %collective-permute-start.3 = (bf16[80,4096]{1,0:T(8,128)(2,1)}, bf16[80,4096]{1,0:T(8,128)(2,1)S(1)}, u32[]{:S(2)}, u32[]{:S(2)}) collective-permute-start(bf16[80,4096]{1,0:T(8,128)(2,1)} %get-tuple-element.24), channel_id=1, source_target_pairs={{0,2},{2,0},{1,3},{3,1},{4,6},{6,4},{5,7},{7,5},{8,10},{10,8},{9,1... | collective-permute-start | bytes 1966088 | tf_op jit(solution)/shard_map/ppermute | solution.py:22
  87.4 97.4 %collective-permute-start.6 = (bf16[8,16,32,128]{3,2,1,0:T(8,128)(2,1)S(1)}, bf16[8,16,32,128]{3,2,1,0:T(8,128)(2,1)S(1)}, u32[]{:S(2)}, u32[]{:S(2)}) collective-permute-start(bf16[8,16,32,128]{3,2,1,0:T(8,128)(2,1)S(1)} %get-tuple-element.13), channel_id=1, source_target_pairs={{0,8},{8,0},{1,9},{9,1},{2,10},{10,2},{3,11},{11,3},{4,12},{12,4},... | collective-permute-start | bytes 3145736 | tf_op jit(solution)/shard_map/ppermute | solution.py:203
  100.4 14.6 %copy-start.4 = (bf16[8,1024,128]{2,1,0:T(8,128)(2,1)S(1)}, bf16[8,1024,128]{2,1,0:T(8,128)(2,1)}, u32[]{:S(2)}) copy-start(bf16[8,1024,128]{2,1,0:T(8,128)(2,1)} %copy-done.3) | copy-start | bytes 6291460
  102.8 9.1 %collective-permute-start.5 = (bf16[40,4096]{1,0:T(8,128)(2,1)S(1)}, bf16[40,4096]{1,0:T(8,128)(2,1)S(1)}, u32[]{:S(2)}, u32[]{:S(2)}) collective-permute-start(bf16[40,4096]{1,0:T(8,128)(2,1)S(1)} %slice.123), channel_id=1, source_target_pairs={{0,1},{1,0},{2,3},{3,2},{4,5},{5,4},{6,7},{7,6},{8,9},{9,8},{10,11... | collective-permute-start | bytes 983048 | tf_op jit(solution)/shard_map/ppermute | solution.py:22
  105.3 8.8 %collective-permute-start.4 = (bf16[40,4096]{1,0:T(8,128)(2,1)S(1)}, bf16[40,4096]{1,0:T(8,128)(2,1)S(1)}, u32[]{:S(2)}, u32[]{:S(2)}) collective-permute-start(bf16[40,4096]{1,0:T(8,128)(2,1)S(1)} %slice.122), channel_id=1, source_target_pairs={{0,2},{2,0},{1,3},{3,1},{4,6},{6,4},{5,7},{7,5},{8,10},{10,8},{9,1... | collective-permute-start | bytes 983048 | tf_op jit(solution)/shard_map/ppermute | solution.py:22
  122.1 5.8 %copy-start.6 = (bf16[80,8192]{1,0:T(8,128)(2,1)S(1)}, bf16[80,8192]{1,0:T(8,128)(2,1)}, u32[]{:S(2)}) copy-start(bf16[80,8192]{1,0:T(8,128)(2,1)} %copy-done.5) | copy-start | bytes 3932164
  124.9 6.3 %copy-start.17 = (bf16[1024,8,128]{0,2,1:T(8,128)(2,1)S(1)}, bf16[1024,8,128]{0,2,1:T(8,128)(2,1)}, u32[]{:S(2)}) copy-start(bf16[1024,8,128]{0,2,1:T(8,128)(2,1)} %copy.36) | copy-start | bytes 6291460
  124.9 6.3 %copy-start.27 = (pred[320,8]{0,1:T(8,128)(4,1)S(1)}, pred[320,8]{0,1:T(8,128)(4,1)}, u32[]{:S(2)}) copy-start(pred[320,8]{0,1:T(8,128)(4,1)} %get-tuple-element.41) | copy-start | bytes 7684
  128.8 29.2 %collective-permute-start.14 = (bf16[80,4096]{1,0:T(8,128)(2,1)S(1)}, bf16[80,4096]{1,0:T(8,128)(2,1)S(1)}, u32[]{:S(2)}, u32[]{:S(2)}) collective-permute-start(bf16[80,4096]{1,0:T(8,128)(2,1)S(1)} %get-tuple-element.22), channel_id=1, source_target_pairs={{0,1},{1,0},{2,3},{3,2},{4,5},{5,4},{6,7},{7,6},{8,9},{9,8},{10,11... | collective-permute-start | bytes 1966088 | tf_op jit(solution)/shard_map/ppermute | solution.py:22
  129.5 26.8 %collective-permute-start.15 = (bf16[80,4096]{1,0:T(8,128)(2,1)S(1)}, bf16[80,4096]{1,0:T(8,128)(2,1)S(1)}, u32[]{:S(2)}, u32[]{:S(2)}) collective-permute-start(bf16[80,4096]{1,0:T(8,128)(2,1)S(1)} %get-tuple-element.22), channel_id=1, source_target_pairs={{0,2},{2,0},{1,3},{3,1},{4,6},{6,4},{5,7},{7,5},{8,10},{10,8},{9,1... | collective-permute-start | bytes 1966088 | tf_op jit(solution)/shard_map/ppermute | solution.py:22
  133.5 22.7 %collective-permute-start.11 = (f32[2,320,128]{2,1,0:T(8,128)S(1)}, f32[2,320,128]{2,1,0:T(8,128)S(1)}, u32[]{:S(2)}, u32[]{:S(2)}) collective-permute-start(f32[2,320,128]{2,1,0:T(8,128)S(1)} %pad_maximum_fusion.2), channel_id=1, source_target_pairs={{0,4},{4,0},{1,5},{5,1},{2,6},{6,2},{3,7},{7,3},{8,12},{12,8},{9,1... | collective-permute-start | bytes 983048 | tf_op jit(solution)/shard_map/ppermute | solution.py:22
  156.2 10.0 %collective-permute-start.12 = (f32[2,320,128]{2,1,0:T(8,128)S(1)}, f32[2,320,128]{2,1,0:T(8,128)S(1)}, u32[]{:S(2)}, u32[]{:S(2)}) collective-permute-start(f32[2,320,128]{2,1,0:T(8,128)S(1)} %maximum_add_fusion), channel_id=1, source_target_pairs={{0,2},{2,0},{1,3},{3,1},{4,6},{6,4},{5,7},{7,5},{8,10},{10,8},{9,1... | collective-permute-start | bytes 983048 | tf_op jit(solution)/shard_map/ppermute | solution.py:22
  156.3 10.4 %collective-permute-start.17 = (bf16[40,4096]{1,0:T(8,128)(2,1)S(1)}, bf16[40,4096]{1,0:T(8,128)(2,1)S(1)}, u32[]{:S(2)}, u32[]{:S(2)}) collective-permute-start(bf16[40,4096]{1,0:T(8,128)(2,1)S(1)} %slice.130), channel_id=1, source_target_pairs={{0,1},{1,0},{2,3},{3,2},{4,5},{5,4},{6,7},{7,6},{8,9},{9,8},{10,11... | collective-permute-start | bytes 983048 | tf_op jit(solution)/shard_map/ppermute | solution.py:22
  158.0 14.7 %collective-permute-start.16 = (bf16[40,4096]{1,0:T(8,128)(2,1)S(1)}, bf16[40,4096]{1,0:T(8,128)(2,1)S(1)}, u32[]{:S(2)}, u32[]{:S(2)}) collective-permute-start(bf16[40,4096]{1,0:T(8,128)(2,1)S(1)} %slice.129), channel_id=1, source_target_pairs={{0,2},{2,0},{1,3},{3,1},{4,6},{6,4},{5,7},{7,5},{8,10},{10,8},{9,1... | collective-permute-start | bytes 983048 | tf_op jit(solution)/shard_map/ppermute | solution.py:22
  163.6 10.0 %copy-start.8 = (bf16[320,4096]{1,0:T(8,128)(2,1)}, bf16[320,4096]{1,0:T(8,128)(2,1)S(1)}, u32[]{:S(2)}) copy-start(bf16[320,4096]{1,0:T(8,128)(2,1)S(1)} %get-tuple-element.17) | copy-start | bytes 7864324
  163.6 44.6 %collective-permute-start.20 = (bf16[80,4096]{1,0:T(8,128)(2,1)}, bf16[80,4096]{1,0:T(8,128)(2,1)}, u32[]{:S(2)}, u32[]{:S(2)}) collective-permute-start(bf16[80,4096]{1,0:T(8,128)(2,1)} %get-tuple-element.18), channel_id=1, source_target_pairs={{0,1},{1,0},{2,3},{3,2},{4,5},{5,4},{6,7},{7,6},{8,9},{9,8},{10,11... | collective-permute-start | bytes 1966088 | tf_op jit(solution)/shard_map/ppermute | solution.py:22
  165.3 19.5 %copy-start.26 = (bf16[320,8]{0,1:T(8,128)(2,1)S(1)}, bf16[320,8]{0,1:T(8,128)(2,1)}, u32[]{:S(2)}) copy-start(bf16[320,8]{0,1:T(8,128)(2,1)} %get-tuple-element.37) | copy-start | bytes 15364
  166.2 39.8 %collective-permute-start.21 = (bf16[80,4096]{1,0:T(8,128)(2,1)}, bf16[80,4096]{1,0:T(8,128)(2,1)}, u32[]{:S(2)}, u32[]{:S(2)}) collective-permute-start(bf16[80,4096]{1,0:T(8,128)(2,1)} %get-tuple-element.18), channel_id=1, source_target_pairs={{0,2},{2,0},{1,3},{3,1},{4,6},{6,4},{5,7},{7,5},{8,10},{10,8},{9,1... | collective-permute-start | bytes 1966088 | tf_op jit(solution)/shard_map/ppermute | solution.py:22
  166.7 17.8 %collective-permute-start.13 = (f32[2,320,128]{2,1,0:T(8,128)S(1)}, f32[2,320,128]{2,1,0:T(8,128)S(1)}, u32[]{:S(2)}, u32[]{:S(2)}) collective-permute-start(f32[2,320,128]{2,1,0:T(8,128)S(1)} %fusion.156), channel_id=1, source_target_pairs={{0,1},{1,0},{2,3},{3,2},{4,5},{5,4},{6,7},{7,6},{8,9},{9,8},{10,11... | collective-permute-start | bytes 983048 | tf_op jit(solution)/shard_map/ppermute | solution.py:22
  187.9 72.2 %collective-permute-start.26 = (bf16[16,320,128]{2,1,0:T(8,128)(2,1)}, bf16[16,320,128]{2,1,0:T(8,128)(2,1)}, u32[]{:S(2)}, u32[]{:S(2)}) collective-permute-start(bf16[16,320,128]{2,1,0:T(8,128)(2,1)} %fusion.13), channel_id=1, source_target_pairs={{0,4},{4,0},{1,5},{5,1},{2,6},{6,2},{3,7},{7,3},{8,12},{12,8},{9,1... | collective-permute-start | bytes 3932168 | tf_op jit(solution)/shard_map/ppermute | solution.py:22
  196.4 6.0 %copy-start.15 = (bf16[128,2,4096]{2,1,0:T(2,128)(2,1)}, bf16[128,2,4096]{2,1,0:T(2,128)(2,1)S(1)}, u32[]{:S(2)}) copy-start(bf16[128,2,4096]{2,1,0:T(2,128)(2,1)S(1)} %get-tuple-element.26) | copy-start | bytes 6291460
  196.4 6.0 %copy-start.13 = (bf16[128,2,4096]{2,1,0:T(2,128)(2,1)}, bf16[128,2,4096]{2,1,0:T(2,128)(2,1)S(1)}, u32[]{:S(2)}) copy-start(bf16[128,2,4096]{2,1,0:T(2,128)(2,1)S(1)} %get-tuple-element.25) | copy-start | bytes 6291460
  196.4 6.0 %copy-start.11 = (bf16[320,4096]{1,0:T(8,128)(2,1)S(1)}, bf16[320,4096]{1,0:T(8,128)(2,1)}, u32[]{:S(2)}) copy-start(bf16[320,4096]{1,0:T(8,128)(2,1)} %maximum_dynamic-update-slice_fusion.1) | copy-start | bytes 7864324
  205.5 4.7 %copy-start.9 = (bf16[320,4096]{1,0:T(8,128)(2,1)S(1)}, bf16[320,4096]{1,0:T(8,128)(2,1)}, u32[]{:S(2)}) copy-start(bf16[320,4096]{1,0:T(8,128)(2,1)} %copy-done.8) | copy-start | bytes 7864324
  206.0 15.0 %copy-start.16 = (bf16[128,2,4096]{2,1,0:T(2,128)(2,1)S(1)}, bf16[128,2,4096]{2,1,0:T(2,128)(2,1)}, u32[]{:S(2)}) copy-start(bf16[128,2,4096]{2,1,0:T(2,128)(2,1)} %copy-done.15) | copy-start | bytes 6291460
  207.3 7.1 %collective-permute-start.23 = (bf16[40,4096]{1,0:T(8,128)(2,1)S(1)}, bf16[40,4096]{1,0:T(8,128)(2,1)S(1)}, u32[]{:S(2)}, u32[]{:S(2)}) collective-permute-start(bf16[40,4096]{1,0:T(8,128)(2,1)S(1)} %slice.137), channel_id=1, source_target_pairs={{0,1},{1,0},{2,3},{3,2},{4,5},{5,4},{6,7},{7,6},{8,9},{9,8},{10,11... | collective-permute-start | bytes 983048 | tf_op jit(solution)/shard_map/ppermute | solution.py:22
  209.2 11.8 %collective-permute-start.22 = (bf16[40,4096]{1,0:T(8,128)(2,1)S(1)}, bf16[40,4096]{1,0:T(8,128)(2,1)S(1)}, u32[]{:S(2)}, u32[]{:S(2)}) collective-permute-start(bf16[40,4096]{1,0:T(8,128)(2,1)S(1)} %slice.136), channel_id=1, source_target_pairs={{0,2},{2,0},{1,3},{3,1},{4,6},{6,4},{5,7},{7,5},{8,10},{10,8},{9,1... | collective-permute-start | bytes 983048 | tf_op jit(solution)/shard_map/ppermute | solution.py:22
  228.7 27.7 %collective-permute-start.24 = (bf16[2,480,128]{2,1,0:T(8,128)(2,1)S(1)}, bf16[2,480,128]{2,1,0:T(8,128)(2,1)S(1)}, u32[]{:S(2)}, u32[]{:S(2)}) collective-permute-start(bf16[2,480,128]{2,1,0:T(8,128)(2,1)S(1)} %get-tuple-element.31), channel_id=1, source_target_pairs={{0,0},{1,4},{2,1},{3,5},{4,2},{5,6},{6,3},{7,7},{8,8},{9,12},{10,9... | collective-permute-start | bytes 737288 | tf_op jit(solution)/shard_map/ppermute | solution.py:341
  230.7 29.4 %collective-permute-start.25 = (bf16[2,480,128]{2,1,0:T(8,128)(2,1)S(1)}, bf16[2,480,128]{2,1,0:T(8,128)(2,1)S(1)}, u32[]{:S(2)}, u32[]{:S(2)}) collective-permute-start(bf16[2,480,128]{2,1,0:T(8,128)(2,1)S(1)} %get-tuple-element.32), channel_id=1, source_target_pairs={{0,4},{1,0},{2,5},{3,1},{4,6},{5,2},{6,7},{7,3},{8,12},{9,8},{10,1... | collective-permute-start | bytes 737288 | tf_op jit(solution)/shard_map/ppermute | solution.py:344
  255.8 4.3 %copy-start.12 = (f32[16,320,128]{2,1,0:T(8,128)S(1)}, f32[16,320,128]{2,1,0:T(8,128)}, u32[]{:S(2)}) copy-start(f32[16,320,128]{2,1,0:T(8,128)} %fusion.37) | copy-start | bytes 7864324
  (10 other events, 21.5 us)

commit v2 on v1

--- a/solution.py
+++ b/solution.py
@@ -240,6 +240,7 @@
     ).astype(bf)
     near_half = lax.dynamic_slice_in_dim(normed, side * half_width, half_width, 1)
     far_half = lax.dynamic_slice_in_dim(normed, (1 - side) * half_width, half_width, 1)
+    near_half, far_half = lax.optimization_barrier((near_half, far_half))
     other_near = swap(far_half, 2)
     own_near_all, first_in = side_gather(near_half, index)
     zero = (first_in[0, 0] * jnp.zeros((), bf)).astype(jnp.int32)

time: 276 us -> 264 us (0.957)
  starting transfers between devices: 55.7 us -> 31.2 us
  waiting for transfers between devices: 74 us -> 96.2 us
  matrix products: 54.9 us -> 51.7 us
    ppermute x1, starting transfers between devices: 25.2 us -> 1.39 us  [on_square(): lax.ppermute(jnp.where(odd, for_low, for_high), 'tensor', [(c, c // 2 + 4...]
    ppermute x1, waiting for transfers between devices: 0.01 us -> 13 us  [on_square(): lax.ppermute(jnp.where(odd, for_high, for_low), 'tensor', [(c, c // 2 + 4...]
    ppermute x22, waiting for transfers between devices: 70.4 us -> 81.2 us  [partner_2(): return lax.ppermute(block, axis, route)]
    dynamic_update_slice x9 -> x8, local copies, waits for them, and re-layouts: 11.3 us -> 7.55 us  [side_gather(): lax.dynamic_update_slice_in_dim(result, piece, (index ^ mask) * count, 0)]
    dot_general x2, matrix products: 8.7 us -> 5.38 us  [key_values(): jnp.einsum('tf,ckf->ktc', far, kv_far, preferred_element_type=f32)]
    unnamed x63 -> x57, local copies, waits for them, and re-layouts: 11.6 us -> 11.6 us
where the time goes in v2:
time: 264 us; the launch traced here: 263 us
  waiting for transfers between devices  96.2 us (36%)
  matrix products  51.7 us (20%)
  local copies, waits for them, and re-layouts  50.6 us (19%)
  starting transfers between devices  31.2 us (12%)
  other arithmetic  22.5 us (9%)
  Pallas kernels  6.03 us (2%)
  between operations  4.98 us (2%)
    ppermute x22, waiting for transfers between devices, partner_2(): return lax.ppermute(block, axis, route)  81.2 us
    ppermute x22, starting transfers between devices, partner_2(): return lax.ppermute(block, axis, route)  27.2 us
    dot_general x2, matrix products, query_base(): jnp.einsum('tf,mfd->mtd', gathered, query_weight, preferred_element_type=...  22 us
    ppermute x1, waiting for transfers between devices, on_square(): lax.ppermute(jnp.where(odd, for_high, for_low), 'tensor', [(c, c // 2 + 4...  13 us
    unnamed x57, local copies, waits for them, and re-layouts  11.6 us
    dynamic_update_slice x7, other arithmetic, side_gather(): lax.dynamic_update_slice_in_dim(result, piece, (index ^ mask) * count, 0)  8.58 us
    dynamic_update_slice x8, local copies, waits for them, and re-layouts, side_gather(): lax.dynamic_update_slice_in_dim(result, piece, (index ^ mask) * count, 0)  7.55 us
    dot_general x2, matrix products, key_values(): jnp.einsum('tf,ckf->ktc', near, kv_near, preferred_element_type=f32)  7.37 us
  transfers between devices with their start and end apart: 27, of which 12 were waited for; matrix products, arithmetic and copies ran while one was open for 37% of the time, Pallas kernels for 2%

profile of v2, /device:TPU:12, one launch (start us, length us, event | category | flops | bytes accessed | tf_op | source)
XLA Modules:
  0.0 263.2 jit_solution(12470691373765803159)
XLA Ops:
  0.0 1.7 fusion.8
  1.7 1.8 fusion.10
  4.5 1.5 collective-permute-start.1
  6.4 2.6 collective-permute-start
  10.7 26.8 %collective-permute-done = bf16[80,4096]{1,0:T(8,128)(2,1)} collective-permute-done((bf16[80,4096]{1,0:T(8,128)(2,1)S(1)}, bf16[80,4096]{1,0:T(8,128)(2,1)}, u32[]{:S(2)}, u32[]{:S(2)}) %collective-permute-start) | collective-permute-done | bytes 655392 | tf_op jit(solution)/shard_map/ppermute | solution.py:22
  40.8 4.6 %copy-done.1 = bf16[48,1024,128]{2,1,0:T(8,128)(2,1)S(1)} copy-done((bf16[48,1024,128]{2,1,0:T(8,128)(2,1)S(1)}, bf16[48,1024,128]{2,1,0:T(8,128)(2,1)}, u32[]{:S(2)}) %copy-start.1) | copy-done | bytes 12582936
  45.3 2.8 %copy-done.2 = bf16[48,16,32,128]{3,2,1,0:T(8,128)(2,1)S(1)} copy-done((bf16[48,16,32,128]{3,2,1,0:T(8,128)(2,1)S(1)}, bf16[48,16,32,128]{3,2,1,0:T(8,128)(2,1)}, u32[]{:S(2)}) %copy-start.2) | copy-done | bytes 6291480
  48.1 6.0 %shard_map.100 = (bf16[8,1024,128]{2,1,0:T(8,128)(2,1)}, bf16[8,16,32,128]{3,2,1,0:T(8,128)(2,1)S(1)}, bf16[8,64,128]{2,1,0:T(8,128)(2,1)S(1)}, bf16[8,1024,128]...) custom-call(s32[2,8]{1,0:T(2,128)S(1)} %broadcast_add_fusion.4.wanted, ...), custom_call_target="tpu_custom_call" | custom-call | tf_op jit(solution)/shard_map/pallas_call | solution.py:190
  56.5 1.7 slice.125
  61.3 1.8 broadcast.307.clone.1
  63.1 2.3 constant_dynamic-update-slice_fusion.11
  65.4 1.5 collective-permute-start.2
  67.2 2.3 broadcast_add_fusion.1
  72.2 2.0 collective-permute-start.3
  75.4 2.5 collective-permute-start.19
  77.9 2.0 maximum_dynamic-update-slice_fusion.1
  79.8 11.0 %fusion.37 = f32[16,320,128]{2,1,0:T(8,128)} fusion(bf16[16,4096,128]{2,1,0:T(8,128)(2,1)} %param.12, bf16[320,4096]{1,0:T(8,128)(2,1)} %maximum_dynamic-update-slice_fusion.1), kind=kOutput, calls=%fused_computation.43 | convolution fusion | flops 5368709120 | bytes 22020096 | tf_op jit(solution)/shard_map/tf,mfd->mtd/dot_general | solution.py:306
  90.9 12.4 %collective-permute-done.3 = bf16[80,4096]{1,0:T(8,128)(2,1)} collective-permute-done((bf16[80,4096]{1,0:T(8,128)(2,1)}, bf16[80,4096]{1,0:T(8,128)(2,1)}, u32[]{:S(2)}, u32[]{:S(2)}) %collective-permute-start.3) | collective-permute-done | bytes 655392 | tf_op jit(solution)/shard_map/ppermute | solution.py:22
  105.8 2.5 collective-permute-start.4
  108.4 2.0 constant_dynamic-update-slice_fusion.10
  110.4 2.0 constant_dynamic-update-slice_fusion.9
  113.7 2.1 collective-permute-done.4
  116.6 3.3 %select_bitcast_fusion = bf16[1024,8,128]{2,0,1:T(8,128)(2,1)} fusion(bf16[8,1024,128]{2,1,0:T(8,128)(2,1)S(1)} %copy-done.4, bf16[8,1024,128]{2,1,0:T(8,128)(2,1)} %collective-permute-done.10, pred[8]{0:T(512)(128)(4,1)S(1)} %compare_and_fusion.3), kind=kLoop, calls=%fused_computation.37 | loop fusion | flops 1048576 | bytes 6291464 | tf_op jit(solution)/shard_map/transpose | solution.py:274
  119.9 3.9 %copy.36 = bf16[1024,8,128]{0,2,1:T(8,128)(2,1)} copy(bf16[1024,8,128]{2,0,1:T(8,128)(2,1)} %select_bitcast_fusion) | data formatting | bytes 4194304 | tf_op jit(solution)/shard_map/transpose | solution.py:274
  123.9 2.8 %fusion.51 = f32[320,128]{1,0:T(8,128)S(1)} fusion(bf16[1024,8,128]{0,2,1:T(8,128)(2,1)} %copy.36, bf16[320,4096]{1,0:T(8,128)(2,1)} %maximum_dynamic-update-slice_fusion.1, s32[]{:T(128)S(6)} %select_n.167, pred[320,8]{0,1:T(8,128)(4,1)S(1)} %get-tuple-element.47), kind=kOutput, calls=%fused_computation.49 | convolution fusion | flops 671703040 | bytes 2918916 | tf_op jit(solution)/shard_map/dot_general | solution.py:278
  126.7 2.2 fusion.48
  132.7 11.0 %fusion.34 = f32[16,320,128]{2,1,0:T(8,128)} fusion(bf16[16,4096,128]{2,1,0:T(8,128)(2,1)} %param.12, bf16[320,4096]{1,0:T(8,128)(2,1)} %maximum_dynamic-update-slice_fusion), kind=kOutput, calls=%fused_computation.42 | convolution fusion | flops 5368709120 | bytes 22020096 | tf_op jit(solution)/shard_map/tf,mfd->mtd/dot_general | solution.py:306
  145.1 2.5 collective-permute-start.12
  150.2 2.1 constant_dynamic-update-slice_fusion.2
  153.0 15.4 %collective-permute-done.12 = f32[2,320,128]{2,1,0:T(8,128)S(1)} collective-permute-done((f32[2,320,128]{2,1,0:T(8,128)S(1)}, f32[2,320,128]{2,1,0:T(8,128)S(1)}, u32[]{:S(2)}, u32[]{:S(2)}) %collective-permute-start.12) | collective-permute-done | bytes 327712 | tf_op jit(solution)/shard_map/ppermute | solution.py:22
  168.4 1.5 collective-permute-start.13
  172.2 6.7 %collective-permute-done.13 = f32[2,320,128]{2,1,0:T(8,128)S(1)} collective-permute-done((f32[2,320,128]{2,1,0:T(8,128)S(1)}, f32[2,320,128]{2,1,0:T(8,128)S(1)}, u32[]{:S(2)}, u32[]{:S(2)}) %collective-permute-start.13) | collective-permute-done | bytes 327712 | tf_op jit(solution)/shard_map/ppermute | solution.py:22
  178.9 1.7 collective-permute-start.16
  186.3 6.5 %constant_dynamic-slice_fusion.2 = (bf16[128,2,4096]{2,1,0:T(2,128)(2,1)S(1)}, bf16[128,2,4096]{2,1,0:T(2,128)(2,1)S(1)}) fusion(bf16[128,2,8192]{2,1,0:T(2,128)(2,1)} %param.13, s32[]{:T(128)S(6)} %select_n.172, s32[]{:T(128)S(6)} %select_n.173), kind=kLoop, calls=%fused_computation.140 | loop fusion | bytes 8388616 | tf_op jit(solution)/shard_map/dynamic_slice | solution.py:321
  192.9 1.7 collective-permute-done.16
  195.7 2.7 %fusion.16 = f32[128,2,320]{0,2,1:T(8,128)S(1)} fusion(bf16[320,4096]{1,0:T(8,128)(2,1)S(1)} %maximum_dynamic-update-slice_fusion.2, bf16[128,2,4096]{2,1,0:T(2,128)(2,1)S(1)} %get-tuple-element.28), kind=kOutput, calls=%fused_computation.23 | convolution fusion | flops 671088640 | bytes 5046272 | tf_op jit(solution)/shard_map/tf,ckf->ktc/dot_general | solution.py:328
  198.4 2.9 %fusion.69 = f32[2,320,128]{2,1,0:T(8,128)S(1)} fusion(f32[128,2,320]{0,2,1:T(8,128)S(1)} %fusion.16, bf16[320,4096]{1,0:T(8,128)(2,1)S(1)} %copy-done.9, bf16[128,2,4096]{2,1,0:T(2,128)(2,1)S(1)} %get-tuple-element.27), kind=kOutput, calls=%fused_computation.53 | convolution fusion | flops 671170560 | bytes 5373952 | tf_op jit(solution)/shard_map/tf,ckf->ktc/dot_general | solution.py:328
  204.3 2.5 collective-permute-start.22
  209.2 2.6 collective-permute-done.23
  211.7 11.3 %collective-permute-done.22 = bf16[40,4096]{1,0:T(8,128)(2,1)S(1)} collective-permute-done((bf16[40,4096]{1,0:T(8,128)(2,1)S(1)}, bf16[40,4096]{1,0:T(8,128)(2,1)S(1)}, u32[]{:S(2)}, u32[]{:S(2)}) %collective-permute-start.22) | collective-permute-done | bytes 327712 | tf_op jit(solution)/shard_map/ppermute | solution.py:22
  223.1 2.7 %fusion.14 = f32[128,2,320]{0,2,1:T(8,128)S(1)} fusion(bf16[320,4096]{1,0:T(8,128)(2,1)S(1)} %maximum_dynamic-update-slice_fusion.3, bf16[128,2,4096]{2,1,0:T(2,128)(2,1)S(1)} %copy-done.18), kind=kOutput, calls=%fused_computation.21 | convolution fusion | flops 671088640 | bytes 5046272 | tf_op jit(solution)/shard_map/tf,ckf->ktc/dot_general | solution.py:328
  225.8 4.5 %fusion.59 = f32[2,320,128]{2,1,0:T(8,128)S(1)} fusion(f32[128,2,320]{0,2,1:T(8,128)S(1)} %fusion.14, bf16[320,4096]{1,0:T(8,128)(2,1)} %maximum_dynamic-update-slice_fusion, bf16[128,2,4096]{2,1,0:T(2,128)(2,1)S(1)} %copy-done.16), kind=kOutput, calls=%fused_computation.51 | convolution fusion | flops 671170560 | bytes 5373952 | tf_op jit(solution)/shard_map/tf,ckf->ktc/dot_general | solution.py:328
  230.8 2.3 collective-permute-start.24
  235.1 13.0 %collective-permute-done.24 = bf16[2,480,128]{2,1,0:T(8,128)(2,1)S(1)} collective-permute-done((bf16[2,480,128]{2,1,0:T(8,128)(2,1)S(1)}, bf16[2,480,128]{2,1,0:T(8,128)(2,1)S(1)}, u32[]{:S(2)}, u32[]{:S(2)}) %collective-permute-start.24) | collective-permute-done | bytes 245792 | tf_op jit(solution)/shard_map/ppermute | solution.py:342
  248.1 2.0 collective-permute-done.25
  250.3 1.8 fusion.12
  252.1 5.5 %fusion.137 = (f32[2,2,8,160]{3,2,1,0:T(8,128)S(1)}, f32[2,2,8,160,320]{4,3,2,1,0:T(8,128)}) fusion(pred[2,160,320]{2,1,0:T(8,128)(4,1)S(1)} %copy-done.25, bf16[2,8,2,160,128]{4,3,2,1,0:T(8,128)(2,1)S(1)} %bitcast.208, bf16[2,1,2,320,128]{4,3,1,0,2:T(8,128)(2,1)S(1)} %get-tuple-element.34, bf16[2,1,2,320,128]{4,3,1,0,2:T(8,128)(2,1)S(1)} %get-tuple-element.33), kind=kOutput, calls=%fused_computation.180 | convolution fusion | flops 426148160 | bytes 8642560 | tf_op jit(solution)/shard_map/sub | solution.py:373
  257.6 4.5 %fusion.41 = bf16[2,8,2,160,128]{4,3,1,2,0:T(8,128)(2,1)S(1)} fusion(f32[2,2,8,160,320]{4,3,2,1,0:T(8,128)} %get-tuple-element.50, f32[2,2,8,160]{3,2,1,0:T(8,128)S(1)} %get-tuple-element.49, bf16[2,1,2,320,128]{4,3,1,0,2:T(8,128)(2,1)S(1)} %get-tuple-element.33, bf16[2,1,2,320,128]{4,3,1,0,2:T(8,128)(2,1)S(1)} %get-tuple-element.34), kind=kOutput, calls=%fused_computation.45 | convolution fusion | flops 424017920 | bytes 8540160 | tf_op jit(solution)/shard_map/gbhqk,gbkd->ghbqd/dot_general | solution.py:375
  (162 shorter events, 42.9 us)
Async XLA Ops:
  1.7 7.4 %copy-start.27 = (s32[2,8]{1,0:T(2,128)S(1)}, s32[2,8]{1,0:T(2,128)}, u32[]{:S(2)}) copy-start(s32[2,8]{1,0:T(2,128)} %param.19) | copy-start | bytes 196
  1.7 8.7 %copy-start.23 = (bf16[48,8192]{1,0:T(8,128)(2,1)S(1)}, bf16[48,8192]{1,0:T(8,128)(2,1)}, u32[]{:S(2)}) copy-start(bf16[48,8192]{1,0:T(8,128)(2,1)} %param.16) | copy-start | bytes 2359300
  3.5 37.2 %copy-start.26 = (s32[2,8]{1,0:T(2,128)S(1)}, s32[2,8]{1,0:T(2,128)}, u32[]{:S(2)}) copy-start(s32[2,8]{1,0:T(2,128)} %param.17) | copy-start | bytes 196
  3.5 37.3 %copy-start = (s32[96]{0:T(128)S(1)}, s32[96]{0:T(128)}, u32[]{:S(2)}) copy-start(s32[96]{0:T(128)} %slot.1) | copy-start | bytes 1156
  4.5 36.3 %copy-start.12 = (bf16[80,4096]{1,0:T(8,128)(2,1)}, bf16[80,4096]{1,0:T(8,128)(2,1)S(1)}, u32[]{:S(2)}) copy-start(bf16[80,4096]{1,0:T(8,128)(2,1)S(1)} %get-tuple-element.13) | copy-start | bytes 1966084
  4.5 35.0 %collective-permute-start.1 = (bf16[80,4096]{1,0:T(8,128)(2,1)}, bf16[80,4096]{1,0:T(8,128)(2,1)S(1)}, u32[]{:S(2)}, u32[]{:S(2)}) collective-permute-start(bf16[80,4096]{1,0:T(8,128)(2,1)} %get-tuple-element.14), channel_id=1, source_target_pairs={{0,1},{1,0},{2,3},{3,2},{4,5},{5,4},{6,7},{7,6},{8,9},{9,8},{10,11... | collective-permute-start | bytes 1966088 | tf_op jit(solution)/shard_map/ppermute | solution.py:22
  6.0 50.5 %collective-permute-start.7 = (bf16[80,4096]{1,0:T(8,128)(2,1)}, bf16[80,4096]{1,0:T(8,128)(2,1)}, u32[]{:S(2)}, u32[]{:S(2)}) collective-permute-start(bf16[80,4096]{1,0:T(8,128)(2,1)} %get-tuple-element.14), channel_id=1, source_target_pairs={{0,2},{2,0},{1,3},{3,1},{4,6},{6,4},{5,7},{7,5},{8,10},{10,8},{9,1... | collective-permute-start | bytes 1966088 | tf_op jit(solution)/shard_map/ppermute | solution.py:22
  6.4 31.1 %collective-permute-start = (bf16[80,4096]{1,0:T(8,128)(2,1)S(1)}, bf16[80,4096]{1,0:T(8,128)(2,1)}, u32[]{:S(2)}, u32[]{:S(2)}) collective-permute-start(bf16[80,4096]{1,0:T(8,128)(2,1)S(1)} %get-tuple-element.13), channel_id=1, source_target_pairs={{0,4},{4,0},{1,5},{5,1},{2,6},{6,2},{3,7},{7,3},{8,12},{12,8},{9,1... | collective-permute-start | bytes 1966088 | tf_op jit(solution)/shard_map/ppermute | solution.py:22
  40.8 4.6 %copy-start.1 = (bf16[48,1024,128]{2,1,0:T(8,128)(2,1)S(1)}, bf16[48,1024,128]{2,1,0:T(8,128)(2,1)}, u32[]{:S(2)}) copy-start(bf16[48,1024,128]{2,1,0:T(8,128)(2,1)} %refs_0_.1) | copy-start | bytes 37748740
  45.3 2.8 %copy-start.2 = (bf16[48,16,32,128]{3,2,1,0:T(8,128)(2,1)S(1)}, bf16[48,16,32,128]{3,2,1,0:T(8,128)(2,1)}, u32[]{:S(2)}) copy-start(bf16[48,16,32,128]{3,2,1,0:T(8,128)(2,1)} %refs_1_.1) | copy-start | bytes 18874372
  48.1 10.6 %copy-start.21 = (bf16[80,4096]{1,0:T(8,128)(2,1)S(1)}, bf16[80,4096]{1,0:T(8,128)(2,1)}, u32[]{:S(2)}) copy-start(bf16[80,4096]{1,0:T(8,128)(2,1)} %copy-done.20) | copy-start | bytes 1966084
  55.5 61.1 %collective-permute-start.10 = (bf16[8,1024,128]{2,1,0:T(8,128)(2,1)}, bf16[8,1024,128]{2,1,0:T(8,128)(2,1)}, u32[]{:S(2)}, u32[]{:S(2)}) collective-permute-start(bf16[8,1024,128]{2,1,0:T(8,128)(2,1)} %get-tuple-element.15), channel_id=1, source_target_pairs={{0,8},{8,0},{1,9},{9,1},{2,10},{10,2},{3,11},{11,3},{4,12},{12,4},... | collective-permute-start | bytes 6291464 | tf_op jit(solution)/shard_map/ppermute | solution.py:203
  58.2 17.0 %collective-permute-start.9 = (bf16[40,4096]{1,0:T(8,128)(2,1)}, bf16[40,4096]{1,0:T(8,128)(2,1)}, u32[]{:S(2)}, u32[]{:S(2)}) collective-permute-start(bf16[40,4096]{1,0:T(8,128)(2,1)} %slice.125), channel_id=1, source_target_pairs={{0,1},{1,0},{2,3},{3,2},{4,5},{5,4},{6,7},{7,6},{8,9},{9,8},{10,11... | collective-permute-start | bytes 983048 | tf_op jit(solution)/shard_map/ppermute | solution.py:22
  59.5 15.9 %collective-permute-start.8 = (bf16[40,4096]{1,0:T(8,128)(2,1)}, bf16[40,4096]{1,0:T(8,128)(2,1)}, u32[]{:S(2)}, u32[]{:S(2)}) collective-permute-start(bf16[40,4096]{1,0:T(8,128)(2,1)} %slice.124), channel_id=1, source_target_pairs={{0,2},{2,0},{1,3},{3,1},{4,6},{6,4},{5,7},{7,5},{8,10},{10,8},{9,1... | collective-permute-start | bytes 983048 | tf_op jit(solution)/shard_map/ppermute | solution.py:22
  65.4 4.1 %copy-start.22 = (bf16[80,4096]{1,0:T(8,128)(2,1)S(1)}, bf16[80,4096]{1,0:T(8,128)(2,1)}, u32[]{:S(2)}) copy-start(bf16[80,4096]{1,0:T(8,128)(2,1)} %copy-done.20) | copy-start | bytes 1966084
  65.4 39.5 %collective-permute-start.2 = (bf16[80,4096]{1,0:T(8,128)(2,1)}, bf16[80,4096]{1,0:T(8,128)(2,1)}, u32[]{:S(2)}, u32[]{:S(2)}) collective-permute-start(bf16[80,4096]{1,0:T(8,128)(2,1)} %get-tuple-element.26), channel_id=1, source_target_pairs={{0,1},{1,0},{2,3},{3,2},{4,5},{5,4},{6,7},{7,6},{8,9},{9,8},{10,11... | collective-permute-start | bytes 1966088 | tf_op jit(solution)/shard_map/ppermute | solution.py:22
  66.9 3.8 %collective-permute-start.18 = (bf16[8,64,128]{2,1,0:T(8,128)(2,1)S(1)}, bf16[8,64,128]{2,1,0:T(8,128)(2,1)S(1)}, u32[]{:S(2)}, u32[]{:S(2)}) collective-permute-start(bf16[8,64,128]{2,1,0:T(8,128)(2,1)S(1)} %get-tuple-element.20), channel_id=1, source_target_pairs={{0,8},{8,0},{1,9},{9,1},{2,10},{10,2},{3,11},{11,3},{4,12},{12,4},... | collective-permute-start | bytes 393224 | tf_op jit(solution)/shard_map/ppermute | solution.py:203
  72.2 31.0 %collective-permute-start.3 = (bf16[80,4096]{1,0:T(8,128)(2,1)}, bf16[80,4096]{1,0:T(8,128)(2,1)}, u32[]{:S(2)}, u32[]{:S(2)}) collective-permute-start(bf16[80,4096]{1,0:T(8,128)(2,1)} %get-tuple-element.26), channel_id=1, source_target_pairs={{0,2},{2,0},{1,3},{3,1},{4,6},{6,4},{5,7},{7,5},{8,10},{10,8},{9,1... | collective-permute-start | bytes 1966088 | tf_op jit(solution)/shard_map/ppermute | solution.py:22
  75.2 105.7 %collective-permute-start.6 = (bf16[8,16,32,128]{3,2,1,0:T(8,128)(2,1)S(1)}, bf16[8,16,32,128]{3,2,1,0:T(8,128)(2,1)S(1)}, u32[]{:S(2)}, u32[]{:S(2)}) collective-permute-start(bf16[8,16,32,128]{3,2,1,0:T(8,128)(2,1)S(1)} %get-tuple-element.17), channel_id=1, source_target_pairs={{0,8},{8,0},{1,9},{9,1},{2,10},{10,2},{3,11},{11,3},{4,12},{12,4},... | collective-permute-start | bytes 3145736 | tf_op jit(solution)/shard_map/ppermute | solution.py:203
  75.4 74.5 %collective-permute-start.19 = (bf16[80,4096]{1,0:T(8,128)(2,1)}, bf16[80,4096]{1,0:T(8,128)(2,1)}, u32[]{:S(2)}, u32[]{:S(2)}) collective-permute-start(bf16[80,4096]{1,0:T(8,128)(2,1)} %get-tuple-element.31), channel_id=1, source_target_pairs={{0,4},{4,0},{1,5},{5,1},{2,6},{6,2},{3,7},{7,3},{8,12},{12,8},{9,1... | collective-permute-start | bytes 1966088 | tf_op jit(solution)/shard_map/ppermute | solution.py:22
  90.9 25.8 %copy-start.4 = (bf16[8,1024,128]{2,1,0:T(8,128)(2,1)S(1)}, bf16[8,1024,128]{2,1,0:T(8,128)(2,1)}, u32[]{:S(2)}) copy-start(bf16[8,1024,128]{2,1,0:T(8,128)(2,1)} %copy-done.3) | copy-start | bytes 6291460
  104.2 9.4 %collective-permute-start.5 = (bf16[40,4096]{1,0:T(8,128)(2,1)S(1)}, bf16[40,4096]{1,0:T(8,128)(2,1)S(1)}, u32[]{:S(2)}, u32[]{:S(2)}) collective-permute-start(bf16[40,4096]{1,0:T(8,128)(2,1)S(1)} %slice.123), channel_id=1, source_target_pairs={{0,1},{1,0},{2,3},{3,2},{4,5},{5,4},{6,7},{7,6},{8,9},{9,8},{10,11... | collective-permute-start | bytes 983048 | tf_op jit(solution)/shard_map/ppermute | solution.py:22
  105.8 9.9 %collective-permute-start.4 = (bf16[40,4096]{1,0:T(8,128)(2,1)S(1)}, bf16[40,4096]{1,0:T(8,128)(2,1)S(1)}, u32[]{:S(2)}, u32[]{:S(2)}) collective-permute-start(bf16[40,4096]{1,0:T(8,128)(2,1)S(1)} %slice.122), channel_id=1, source_target_pairs={{0,2},{2,0},{1,3},{3,1},{4,6},{6,4},{5,7},{7,5},{8,10},{10,8},{9,1... | collective-permute-start | bytes 983048 | tf_op jit(solution)/shard_map/ppermute | solution.py:22
  123.9 2.8 %copy-start.19 = (bf16[1024,8,128]{0,2,1:T(8,128)(2,1)S(1)}, bf16[1024,8,128]{0,2,1:T(8,128)(2,1)}, u32[]{:S(2)}) copy-start(bf16[1024,8,128]{0,2,1:T(8,128)(2,1)} %copy.36) | copy-start | bytes 6291460
  128.9 3.0 %copy-start.13 = (bf16[80,4096]{1,0:T(8,128)(2,1)S(1)}, bf16[80,4096]{1,0:T(8,128)(2,1)}, u32[]{:S(2)}) copy-start(bf16[80,4096]{1,0:T(8,128)(2,1)} %copy-done.12) | copy-start | bytes 1966084
  129.6 15.5 %collective-permute-start.11 = (f32[2,320,128]{2,1,0:T(8,128)S(1)}, f32[2,320,128]{2,1,0:T(8,128)S(1)}, u32[]{:S(2)}, u32[]{:S(2)}) collective-permute-start(f32[2,320,128]{2,1,0:T(8,128)S(1)} %pad_maximum_fusion.2), channel_id=1, source_target_pairs={{0,4},{4,0},{1,5},{5,1},{2,6},{6,2},{3,7},{7,3},{8,12},{12,8},{9,1... | collective-permute-start | bytes 983048 | tf_op jit(solution)/shard_map/ppermute | solution.py:22
  132.1 16.4 %collective-permute-start.14 = (bf16[80,4096]{1,0:T(8,128)(2,1)S(1)}, bf16[80,4096]{1,0:T(8,128)(2,1)S(1)}, u32[]{:S(2)}, u32[]{:S(2)}) collective-permute-start(bf16[80,4096]{1,0:T(8,128)(2,1)S(1)} %get-tuple-element.24), channel_id=1, source_target_pairs={{0,1},{1,0},{2,3},{3,2},{4,5},{5,4},{6,7},{7,6},{8,9},{9,8},{10,11... | collective-permute-start | bytes 1966088 | tf_op jit(solution)/shard_map/ppermute | solution.py:22
  143.7 26.3 %collective-permute-start.15 = (bf16[80,4096]{1,0:T(8,128)(2,1)S(1)}, bf16[80,4096]{1,0:T(8,128)(2,1)S(1)}, u32[]{:S(2)}, u32[]{:S(2)}) collective-permute-start(bf16[80,4096]{1,0:T(8,128)(2,1)S(1)} %get-tuple-element.24), channel_id=1, source_target_pairs={{0,2},{2,0},{1,3},{3,1},{4,6},{6,4},{5,7},{7,5},{8,10},{10,8},{9,1... | collective-permute-start | bytes 1966088 | tf_op jit(solution)/shard_map/ppermute | solution.py:22
  145.1 23.3 %collective-permute-start.12 = (f32[2,320,128]{2,1,0:T(8,128)S(1)}, f32[2,320,128]{2,1,0:T(8,128)S(1)}, u32[]{:S(2)}, u32[]{:S(2)}) collective-permute-start(f32[2,320,128]{2,1,0:T(8,128)S(1)} %maximum_add_fusion), channel_id=1, source_target_pairs={{0,2},{2,0},{1,3},{3,1},{4,6},{6,4},{5,7},{7,5},{8,10},{10,8},{9,1... | collective-permute-start | bytes 983048 | tf_op jit(solution)/shard_map/ppermute | solution.py:22
  152.2 19.9 %copy-start.6 = (bf16[320,4096]{1,0:T(8,128)(2,1)}, bf16[320,4096]{1,0:T(8,128)(2,1)S(1)}, u32[]{:S(2)}) copy-start(bf16[320,4096]{1,0:T(8,128)(2,1)S(1)} %get-tuple-element.21) | copy-start | bytes 7864324
  152.2 51.1 %collective-permute-start.20 = (bf16[80,4096]{1,0:T(8,128)(2,1)}, bf16[80,4096]{1,0:T(8,128)(2,1)}, u32[]{:S(2)}, u32[]{:S(2)}) collective-permute-start(bf16[80,4096]{1,0:T(8,128)(2,1)} %get-tuple-element.22), channel_id=1, source_target_pairs={{0,1},{1,0},{2,3},{3,2},{4,5},{5,4},{6,7},{7,6},{8,9},{9,8},{10,11... | collective-permute-start | bytes 1966088 | tf_op jit(solution)/shard_map/ppermute | solution.py:22
  152.8 49.1 %collective-permute-start.21 = (bf16[80,4096]{1,0:T(8,128)(2,1)}, bf16[80,4096]{1,0:T(8,128)(2,1)}, u32[]{:S(2)}, u32[]{:S(2)}) collective-permute-start(bf16[80,4096]{1,0:T(8,128)(2,1)} %get-tuple-element.22), channel_id=1, source_target_pairs={{0,2},{2,0},{1,3},{3,1},{4,6},{6,4},{5,7},{7,5},{8,10},{10,8},{9,1... | collective-permute-start | bytes 1966088 | tf_op jit(solution)/shard_map/ppermute | solution.py:22
  168.4 10.4 %collective-permute-start.13 = (f32[2,320,128]{2,1,0:T(8,128)S(1)}, f32[2,320,128]{2,1,0:T(8,128)S(1)}, u32[]{:S(2)}, u32[]{:S(2)}) collective-permute-start(f32[2,320,128]{2,1,0:T(8,128)S(1)} %fusion.156), channel_id=1, source_target_pairs={{0,1},{1,0},{2,3},{3,2},{4,5},{5,4},{6,7},{7,6},{8,9},{9,8},{10,11... | collective-permute-start | bytes 983048 | tf_op jit(solution)/shard_map/ppermute | solution.py:22
  170.7 22.1 %collective-permute-start.17 = (bf16[40,4096]{1,0:T(8,128)(2,1)}, bf16[40,4096]{1,0:T(8,128)(2,1)}, u32[]{:S(2)}, u32[]{:S(2)}) collective-permute-start(bf16[40,4096]{1,0:T(8,128)(2,1)} %slice.130), channel_id=1, source_target_pairs={{0,1},{1,0},{2,3},{3,2},{4,5},{5,4},{6,7},{7,6},{8,9},{9,8},{10,11... | collective-permute-start | bytes 983048 | tf_op jit(solution)/shard_map/ppermute | solution.py:22
  172.2 6.7 %copy-start.10 = (bf16[320,4096]{1,0:T(8,128)(2,1)}, bf16[320,4096]{1,0:T(8,128)(2,1)S(1)}, u32[]{:S(2)}) copy-start(bf16[320,4096]{1,0:T(8,128)(2,1)S(1)} %constant_dynamic-update-slice_fusion.3) | copy-start | bytes 7864324
  178.9 15.7 %collective-permute-start.16 = (bf16[40,4096]{1,0:T(8,128)(2,1)}, bf16[40,4096]{1,0:T(8,128)(2,1)}, u32[]{:S(2)}, u32[]{:S(2)}) collective-permute-start(bf16[40,4096]{1,0:T(8,128)(2,1)} %slice.129), channel_id=1, source_target_pairs={{0,2},{2,0},{1,3},{3,1},{4,6},{6,4},{5,7},{7,5},{8,10},{10,8},{9,1... | collective-permute-start | bytes 983048 | tf_op jit(solution)/shard_map/ppermute | solution.py:22
  183.9 66.4 %collective-permute-start.26 = (bf16[16,320,128]{2,1,0:T(8,128)(2,1)}, bf16[16,320,128]{2,1,0:T(8,128)(2,1)}, u32[]{:S(2)}, u32[]{:S(2)}) collective-permute-start(bf16[16,320,128]{2,1,0:T(8,128)(2,1)} %fusion.13), channel_id=1, source_target_pairs={{0,4},{4,0},{1,5},{5,1},{2,6},{6,2},{3,7},{7,3},{8,12},{12,8},{9,1... | collective-permute-start | bytes 3932168 | tf_op jit(solution)/shard_map/ppermute | solution.py:22
  186.3 8.2 %copy-start.11 = (bf16[320,4096]{1,0:T(8,128)(2,1)S(1)}, bf16[320,4096]{1,0:T(8,128)(2,1)}, u32[]{:S(2)}) copy-start(bf16[320,4096]{1,0:T(8,128)(2,1)} %copy-done.10) | copy-start | bytes 7864324
  192.8 5.5 %copy-start.17 = (bf16[128,2,4096]{2,1,0:T(2,128)(2,1)}, bf16[128,2,4096]{2,1,0:T(2,128)(2,1)S(1)}, u32[]{:S(2)}) copy-start(bf16[128,2,4096]{2,1,0:T(2,128)(2,1)S(1)} %get-tuple-element.28) | copy-start | bytes 6291460
  192.8 5.5 %copy-start.15 = (bf16[128,2,4096]{2,1,0:T(2,128)(2,1)}, bf16[128,2,4096]{2,1,0:T(2,128)(2,1)S(1)}, u32[]{:S(2)}) copy-start(bf16[128,2,4096]{2,1,0:T(2,128)(2,1)S(1)} %get-tuple-element.27) | copy-start | bytes 6291460
  198.4 3.1 %copy-start.24 = (bf16[8,128,64]{2,1,0:T(8,128)(2,1)S(1)}, bf16[8,128,64]{2,1,0:T(8,128)(2,1)}, u32[]{:S(2)}) copy-start(bf16[8,128,64]{2,1,0:T(8,128)(2,1)} %reshape.440) | copy-start | bytes 393220
  201.4 5.4 %copy-start.7 = (bf16[320,4096]{1,0:T(8,128)(2,1)S(1)}, bf16[320,4096]{1,0:T(8,128)(2,1)}, u32[]{:S(2)}) copy-start(bf16[320,4096]{1,0:T(8,128)(2,1)} %copy-done.6) | copy-start | bytes 7864324
  201.9 21.2 %copy-start.18 = (bf16[128,2,4096]{2,1,0:T(2,128)(2,1)S(1)}, bf16[128,2,4096]{2,1,0:T(2,128)(2,1)}, u32[]{:S(2)}) copy-start(bf16[128,2,4096]{2,1,0:T(2,128)(2,1)} %copy-done.17) | copy-start | bytes 6291460
  203.2 8.5 %collective-permute-start.23 = (bf16[40,4096]{1,0:T(8,128)(2,1)S(1)}, bf16[40,4096]{1,0:T(8,128)(2,1)S(1)}, u32[]{:S(2)}, u32[]{:S(2)}) collective-permute-start(bf16[40,4096]{1,0:T(8,128)(2,1)S(1)} %slice.137), channel_id=1, source_target_pairs={{0,1},{1,0},{2,3},{3,2},{4,5},{5,4},{6,7},{7,6},{8,9},{9,8},{10,11... | collective-permute-start | bytes 983048 | tf_op jit(solution)/shard_map/ppermute | solution.py:22
  204.3 18.7 %collective-permute-start.22 = (bf16[40,4096]{1,0:T(8,128)(2,1)S(1)}, bf16[40,4096]{1,0:T(8,128)(2,1)S(1)}, u32[]{:S(2)}, u32[]{:S(2)}) collective-permute-start(bf16[40,4096]{1,0:T(8,128)(2,1)S(1)} %slice.136), channel_id=1, source_target_pairs={{0,2},{2,0},{1,3},{3,1},{4,6},{6,4},{5,7},{7,5},{8,10},{10,8},{9,1... | collective-permute-start | bytes 983048 | tf_op jit(solution)/shard_map/ppermute | solution.py:22
  230.8 17.4 %collective-permute-start.24 = (bf16[2,480,128]{2,1,0:T(8,128)(2,1)S(1)}, bf16[2,480,128]{2,1,0:T(8,128)(2,1)S(1)}, u32[]{:S(2)}, u32[]{:S(2)}) collective-permute-start(bf16[2,480,128]{2,1,0:T(8,128)(2,1)S(1)} %get-tuple-element.37), channel_id=1, source_target_pairs={{0,0},{1,4},{2,1},{3,5},{4,2},{5,6},{6,3},{7,7},{8,8},{9,12},{10,9... | collective-permute-start | bytes 737288 | tf_op jit(solution)/shard_map/ppermute | solution.py:342
  233.1 17.0 %collective-permute-start.25 = (bf16[2,480,128]{2,1,0:T(8,128)(2,1)S(1)}, bf16[2,480,128]{2,1,0:T(8,128)(2,1)S(1)}, u32[]{:S(2)}, u32[]{:S(2)}) collective-permute-start(bf16[2,480,128]{2,1,0:T(8,128)(2,1)S(1)} %get-tuple-element.38), channel_id=1, source_target_pairs={{0,4},{1,0},{2,5},{3,1},{4,6},{5,2},{6,7},{7,3},{8,12},{9,8},{10,1... | collective-permute-start | bytes 737288 | tf_op jit(solution)/shard_map/ppermute | solution.py:345
  234.5 15.8 %copy-start.14 = (f32[16,320,128]{2,1,0:T(8,128)S(1)}, f32[16,320,128]{2,1,0:T(8,128)}, u32[]{:S(2)}) copy-start(f32[16,320,128]{2,1,0:T(8,128)} %fusion.37) | copy-start | bytes 7864324
  (7 other events, 13.0 us)
